TPU v7x, 32 devices: a whole 2x2x4 slice. The times are simulated.
32 devices in a mesh: row: 16 (over z, y, core), col: 2 (over x).
Axes of the slice: x: 2, y: 2, z: 4, core: 2. Of those that a mesh axis runs over, the one named last changes fastest.
Arguments:
- activation: bfloat16 [1024, 1024, 128], P('row', 'col'), may hold values from -6 to 6
- kernel_one: bfloat16 [3, 3, 128, 128], replicated, may hold values from -0.1875 to 0.1875
- bias_one: float32 [128], replicated, may hold values from -0.5 to 0.5
- kernel_two: bfloat16 [3, 3, 128, 128], replicated, may hold values from -0.1875 to 0.1875
- bias_two: float32 [128], replicated, may hold values from -0.5 to 0.5
Outputs:
- result_map: bfloat16 [1024, 1024, 128], P('row', 'col')
All inputs are finite; a program needn't handle non-finite values.
Results may differ from a plain program's by a relative error of at most 0.0095.
Values may be sent and summed in bfloat16 or wider, within the bound.
No kernel may reach another device: no remote copies, remote signals or barrier semaphores. Data moves between devices by JAX's collectives and lax.ppermute only.
A program may use at most 128 MiB of HBM per device.

v0:
```python
import jax
import jax.numpy as jnp
from jax import lax
from jax.sharding import PartitionSpec as P


def with_halo(block, sides, width):
    for axis, dim in sides:
        count = lax.axis_size(axis)
        forward = [(i, i + 1) for i in range(count - 1)]
        backward = [(target, source) for source, target in forward]
        low = lax.ppermute(
            lax.slice_in_dim(block, block.shape[dim] - width, None, axis=dim), axis, forward
        )
        high = lax.ppermute(lax.slice_in_dim(block, 0, width, axis=dim), axis, backward)
        block = jnp.concatenate([low, block, high], axis=dim)
    return block


def dilated(source_map, kernel, offset):
    result = lax.conv_general_dilated(
        source_map[None],
        kernel,
        (1, 1),
        "VALID",
        rhs_dilation=(4, 4),
        dimension_numbers=("NHWC", "HWIO", "NHWC"),
        preferred_element_type=jnp.float32,
    )[0]
    return result + offset


def body(activation, kernel_one, bias_one, kernel_two, bias_two):
    tile_rows, tile_cols, channels = activation.shape
    block_count = lax.axis_size("row") // lax.axis_size("col")
    padded_in = with_halo(activation, (("row", 0), ("col", 1)), 4)
    elu_out = jax.nn.elu(dilated(padded_in, kernel_one, bias_one)).astype(jnp.bfloat16)
    blocks = elu_out.reshape(tile_rows, block_count, tile_rows, channels).transpose(1, 2, 0, 3)
    blocks = blocks.reshape(block_count, tile_rows * tile_rows, channels)
    step_one = lax.all_to_all(blocks, "col", split_axis=1, concat_axis=0, tiled=True)
    step_two = lax.all_to_all(step_one, "row", split_axis=0, concat_axis=0, tiled=True)
    landed = lax.all_to_all(step_two, "col", split_axis=0, concat_axis=1, tiled=True)
    mirrored = landed.reshape(block_count, tile_rows, tile_rows, channels).transpose(1, 0, 2, 3)
    mirrored = mirrored.reshape(tile_rows, tile_cols, channels)
    symmetric = (0.5 * (elu_out.astype(jnp.float32) + mirrored.astype(jnp.float32))).astype(
        jnp.bfloat16
    )
    padded_sym = with_halo(symmetric, (("row", 0), ("col", 1)), 4)
    result_map = symmetric.astype(jnp.float32) + dilated(padded_sym, kernel_two, bias_two)
    return result_map.astype(jnp.bfloat16)


def solution(mesh):
    in_specs = (P("row", "col", None), P(), P(), P(), P())
    out_specs = P("row", "col", None)
    return jax.shard_map(body, mesh=mesh, in_specs=in_specs, out_specs=out_specs, check_vma=False)
```

profile of v0, /device:TPU:16, one launch (start us, length us, event | category | flops | bytes accessed | tf_op | source)
XLA Modules:
  0.0 651.3 jit_solution(13090929127386446977)
XLA Ops:
  0.0 12.2 %copy.32 = bf16[64,512,128]{2,0,1:T(8,128)(2,1)} copy(bf16[64,512,128]{2,1,0:T(8,128)(2,1)} %param.5) | data formatting | bytes 16777216 | tf_op args[0]
  12.2 2.1 fusion.38
  14.3 2.2 collective-permute-start
  16.5 4.5 collective-permute-start.1
  21.1 5.0 collective-permute-done
  28.7 3.4 collective-permute-start.2
  34.1 4.3 collective-permute-done.3
  38.4 11.8 %pad_maximum_fusion = bf16[72,520,128]{2,0,1:T(8,128)(2,1)} fusion(bf16[72,4,128]{2,0,1:T(8,128)(2,1)S(1)} %collective-permute-done.3, bf16[4,512,128]{2,0,1:T(4,128)(2,1)S(1)} %collective-permute-done.1, bf16[64,512,128]{2,0,1:T(8,128)(2,1)S(1)} %copy-done.4, bf16[4,512,128]{2,0,1:T(4,128)(2,1)S(1)} %collective-permute-done, ...), kind=kLoop, calls=%fused_computation.31 | loop fusion | flops 47923200 | bytes 19169280 | tf_op jit(solution)/shard_map/concatenate | solution.py:16
  50.2 8.6 %copy.36 = bf16[72,1,8,65,128]{4,2,3,0,1:T(8,128)(2,1)} copy(bf16[72,1,8,65,128]{4,0,3,2,1:T(8,128)(2,1)} %bitcast.58) | data formatting | bytes 19169280 | tf_op jit(solution)/shard_map/conv_general_dilated | solution.py:21
  60.4 22.5 %broadcast_select_fusion.1 = f32[64,8,65,128]{3,1,2,0:T(8,128)S(1)} fusion(pred[8,65]{0,1:T(8,128)(4,1)S(1)} %copy-done.8, bf16[3,3,128,128]{3,2,1,0:T(8,128)(2,1)S(1)} %copy-done, bf16[72,1,7,8,128]{4,2,3,0,1:T(8,128)(2,1)S(1)} %slice.38, bf16[72,1,8,65,128]{4,2,3,0,1:T(8,128)(2,1)} %copy.36), kind=kOutput, calls=%fused_computation.34 | convolution fusion | flops 9851224064 | bytes 27951624 | tf_op jit(solution)/shard_map/conv_general_dilated | solution.py:21
  82.9 5.3 copy.37
  88.2 2.9 slice.39
  91.1 4.2 copy-done.2
  95.3 7.1 %fusion.5 = bf16[64,8,64,128]{3,0,2,1:T(8,128)(2,1)S(1)} fusion(f32[64,8,64,128]{3,0,2,1:T(8,128)S(1)} %bitcast.57, f32[128]{0:T(128)S(1)} %copy-done.5), kind=kLoop, calls=%fused_computation.10 | loop fusion | flops 20971520 | bytes 25166336 | tf_op jit(solution)/shard_map/convert_element_type | solution.py:37
  102.4 24.6 %copy.38 = bf16[8,4096,128]{2,0,1:T(8,128)(2,1)S(1)} copy(bf16[8,4096,128]{2,1,0:T(8,128)(2,1)S(1)} %bitcast.61) | data formatting | bytes 16777216 | tf_op jit(solution)/shard_map/reshape | solution.py:39
  127.0 96.8 %all_to_all.35 = bf16[8,4096,128]{2,0,1:T(8,128)(2,1)} all-to-all(bf16[8,4096,128]{2,0,1:T(8,128)(2,1)S(1)} %copy.38), channel_id=1, replica_groups=mesh['row'=16,'col'=2] {'col'}, dimensions={1} | all-to-all | bytes 16777216 | tf_op jit(solution)/shard_map/all_to_all | solution.py:40
  223.8 8.3 %copy.40 = bf16[2,8,2048,128]{3,2,1,0:T(8,128)(2,1)} copy(bf16[2,8,2048,128]{3,1,2,0:T(8,128)(2,1)} %bitcast.62) | data formatting | bytes 16777216 | tf_op jit(solution)/shard_map/all_to_all | solution.py:40
  232.0 188.7 %all_to_all.36 = bf16[16,2048,128]{2,1,0:T(8,128)(2,1)S(1)} all-to-all(bf16[16,2048,128]{2,1,0:T(8,128)(2,1)} %bitcast.63), channel_id=1, replica_groups=mesh['row'=16,'col'=2] {'row'}, dimensions={0} | all-to-all | bytes 16777216 | tf_op jit(solution)/shard_map/all_to_all | solution.py:41
  420.7 96.6 %all_to_all.37 = bf16[16,2048,128]{2,1,0:T(8,128)(2,1)} all-to-all(bf16[16,2048,128]{2,1,0:T(8,128)(2,1)S(1)} %all_to_all.36), channel_id=1, replica_groups=mesh['row'=16,'col'=2] {'col'}, dimensions={0} | all-to-all | bytes 16777216 | tf_op jit(solution)/shard_map/all_to_all | solution.py:42
  517.3 10.8 %copy.41 = f32[2,8,2048,128]{3,2,0,1:T(8,128)} copy(bf16[2,8,2048,128]{3,2,1,0:T(8,128)(2,1)} %bitcast.60) | data formatting | bytes 25165824 | tf_op jit(solution)/shard_map/convert_element_type | solution.py:45
  528.1 15.2 %copy.42 = f32[64,8,64,128]{3,0,2,1:T(8,128)S(1)} copy(f32[64,8,64,128]{3,2,0,1:T(8,128)} %bitcast.56) | data formatting | bytes 33554432 | tf_op jit(solution)/shard_map/convert_element_type | solution.py:45
  543.3 11.3 %fusion.10 = bf16[64,512,128]{2,0,1:T(8,128)(2,1)S(1)} fusion(f32[64,8,64,128]{3,0,2,1:T(8,128)S(1)} %copy.42, f32[128]{0:T(128)S(1)} %copy-done.5, f32[64,1,520,128]{3,0,2,1:T(8,128)} %bitcast.52), kind=kLoop, calls=%fused_computation.17 | loop fusion | flops 37748736 | bytes 41943552 | tf_op jit(solution)/shard_map/convert_element_type | solution.py:45
  557.0 4.5 collective-permute-start.5
  561.6 5.0 collective-permute-done.4
  568.3 2.2 collective-permute-start.6
  572.5 4.4 collective-permute-done.7
  576.9 12.2 %pad_maximum_fusion.1 = bf16[72,520,128]{2,0,1:T(8,128)(2,1)} fusion(bf16[72,4,128]{2,0,1:T(8,128)(2,1)S(1)} %collective-permute-done.7, bf16[4,512,128]{2,0,1:T(4,128)(2,1)S(1)} %collective-permute-done.5, bf16[64,512,128]{2,0,1:T(8,128)(2,1)S(1)} %fusion.10, bf16[4,512,128]{2,0,1:T(4,128)(2,1)S(1)} %collective-permute-done.4, ...), kind=kLoop, calls=%fused_computation.32 | loop fusion | flops 47923200 | bytes 19169280 | tf_op jit(solution)/shard_map/concatenate | solution.py:16
  589.2 8.6 %copy.44 = bf16[72,1,8,65,128]{4,2,3,0,1:T(8,128)(2,1)} copy(bf16[72,1,8,65,128]{4,0,3,2,1:T(8,128)(2,1)} %bitcast.59) | data formatting | bytes 19169280 | tf_op jit(solution)/shard_map/conv_general_dilated | solution.py:21
  599.6 24.6 %broadcast_select_fusion = f32[64,8,65,128]{3,1,2,0:T(8,128)} fusion(pred[8,65]{0,1:T(8,128)(4,1)S(1)} %copy-done.8, bf16[3,3,128,128]{3,2,1,0:T(8,128)(2,1)S(1)} %copy-done.7, bf16[72,1,7,8,128]{4,2,3,0,1:T(8,128)(2,1)S(1)} %slice.42, bf16[72,1,8,65,128]{4,2,3,0,1:T(8,128)(2,1)} %copy.44), kind=kOutput, calls=%fused_computation.33 | convolution fusion | flops 9851224064 | bytes 27951624 | tf_op jit(solution)/shard_map/conv_general_dilated | solution.py:21
  624.2 9.5 %copy.45 = f32[64,8,65,128]{3,0,2,1:T(8,128)S(1)} copy(f32[64,8,65,128]{3,1,2,0:T(8,128)} %broadcast_select_fusion) | data formatting | bytes 34078720 | tf_op jit(solution)/shard_map/conv_general_dilated | solution.py:21
  633.8 5.1 fusion.8
  638.9 12.2 %copy.46 = bf16[64,512,128]{2,1,0:T(8,128)(2,1)} copy(bf16[64,512,128]{2,0,1:T(8,128)(2,1)} %fusion.8) | data formatting | bytes 16777216 | tf_op jit(solution)/shard_map/convert_element_type | solution.py:50
  (34 shorter events, 14.1 us)
Async XLA Ops:
  0.0 60.4 %copy-start = (bf16[3,3,128,128]{3,2,1,0:T(8,128)(2,1)S(1)}, bf16[3,3,128,128]{3,2,1,0:T(8,128)(2,1)}, u32[]{:S(2)}) copy-start(bf16[3,3,128,128]{3,2,1,0:T(8,128)(2,1)} %param.6) | copy-start | bytes 884740
  12.2 26.2 %copy-start.4 = (bf16[64,512,128]{2,0,1:T(8,128)(2,1)S(1)}, bf16[64,512,128]{2,0,1:T(8,128)(2,1)}, u32[]{:S(2)}) copy-start(bf16[64,512,128]{2,0,1:T(8,128)(2,1)} %copy.32) | copy-start | bytes 25165828
  14.3 11.8 %collective-permute-start = (bf16[4,512,128]{2,0,1:T(4,128)(2,1)S(1)}, bf16[4,512,128]{2,0,1:T(4,128)(2,1)S(1)}, u32[]{:S(2)}, u32[]{:S(2)}) collective-permute-start(bf16[4,512,128]{2,0,1:T(4,128)(2,1)S(1)} %get-tuple-element.11), channel_id=1, source_target_pairs={{0,2},{2,4},{4,6},{6,8},{8,10},{10,12},{12,14},{14,16},{16,18},{18... | collective-permute-start | bytes 1572872 | tf_op jit(solution)/shard_map/ppermute | solution.py:12
  16.5 11.3 %collective-permute-start.1 = (bf16[4,512,128]{2,0,1:T(4,128)(2,1)S(1)}, bf16[4,512,128]{2,0,1:T(4,128)(2,1)S(1)}, u32[]{:S(2)}, u32[]{:S(2)}) collective-permute-start(bf16[4,512,128]{2,0,1:T(4,128)(2,1)S(1)} %get-tuple-element.12), channel_id=1, source_target_pairs={{2,0},{4,2},{6,4},{8,6},{10,8},{12,10},{14,12},{16,14},{18,16},{20... | collective-permute-start | bytes 1572872 | tf_op jit(solution)/shard_map/ppermute | solution.py:15
  28.7 5.4 collective-permute-start.2
  32.1 28.3 %copy-start.8 = (pred[8,65]{0,1:T(8,128)(4,1)S(1)}, pred[8,65]{0,1:T(8,128)(4,1)}, u32[]{:S(2)}) copy-start(pred[8,65]{0,1:T(8,128)(4,1)} %constant.13) | copy-start | bytes 1564
  32.1 6.2 collective-permute-start.3
  88.2 7.1 %copy-start.2 = (f32[64,8,65,128]{3,0,2,1:T(8,128)}, f32[64,8,65,128]{3,0,2,1:T(8,128)S(1)}, u32[]{:S(2)}) copy-start(f32[64,8,65,128]{3,0,2,1:T(8,128)S(1)} %copy.37) | copy-start | bytes 51118084
  88.2 7.1 %copy-start.5 = (f32[128]{0:T(128)S(1)}, f32[128]{0:T(128)}, u32[]{:S(2)}) copy-start(f32[128]{0:T(128)} %param.7) | copy-start | bytes 1540
  554.7 22.3 %copy-start.3 = (bf16[64,512,128]{2,0,1:T(8,128)(2,1)}, bf16[64,512,128]{2,0,1:T(8,128)(2,1)S(1)}, u32[]{:S(2)}) copy-start(bf16[64,512,128]{2,0,1:T(8,128)(2,1)S(1)} %fusion.10) | copy-start | bytes 25165828
  555.1 11.5 %collective-permute-start.4 = (bf16[4,512,128]{2,0,1:T(4,128)(2,1)S(1)}, bf16[4,512,128]{2,0,1:T(4,128)(2,1)S(1)}, u32[]{:S(2)}, u32[]{:S(2)}) collective-permute-start(bf16[4,512,128]{2,0,1:T(4,128)(2,1)S(1)} %get-tuple-element.9), channel_id=1, source_target_pairs={{0,2},{2,4},{4,6},{6,8},{8,10},{10,12},{12,14},{14,16},{16,18},{18... | collective-permute-start | bytes 1572872 | tf_op jit(solution)/shard_map/ppermute | solution.py:12
  557.0 11.3 %collective-permute-start.5 = (bf16[4,512,128]{2,0,1:T(4,128)(2,1)S(1)}, bf16[4,512,128]{2,0,1:T(4,128)(2,1)S(1)}, u32[]{:S(2)}, u32[]{:S(2)}) collective-permute-start(bf16[4,512,128]{2,0,1:T(4,128)(2,1)S(1)} %get-tuple-element.10), channel_id=1, source_target_pairs={{2,0},{4,2},{6,4},{8,6},{10,8},{12,10},{14,12},{16,14},{18,16},{20... | collective-permute-start | bytes 1572872 | tf_op jit(solution)/shard_map/ppermute | solution.py:15
  568.3 4.2 collective-permute-start.6
  570.6 29.1 %copy-start.7 = (bf16[3,3,128,128]{3,2,1,0:T(8,128)(2,1)S(1)}, bf16[3,3,128,128]{3,2,1,0:T(8,128)(2,1)}, u32[]{:S(2)}) copy-start(bf16[3,3,128,128]{3,2,1,0:T(8,128)(2,1)} %param.8) | copy-start | bytes 884740
  570.6 6.4 collective-permute-start.7
  597.8 35.9 %slice-start = ((s8[8388608]{0:T(1024)(128)(4,1)}), s8[4194304]{0:T(1024)(128)(4,1)S(1)}, s32[]{:S(2)}) async-start(s8[8388608]{0:T(1024)(128)(4,1)} %bitcast.53), calls=%async_computation.3 | async-start | bytes 8388608
  599.6 34.1 %slice-start.1 = ((s8[8388608]{0:T(1024)(128)(4,1)}), s8[4194304]{0:T(1024)(128)(4,1)S(1)}, s32[]{:S(2)}) async-start(s8[8388608]{0:T(1024)(128)(4,1)} %bitcast.53), calls=%async_computation.4 | async-start | bytes 8388608
  624.2 9.6 %copy-start.6 = (f32[128]{0:T(128)S(1)}, f32[128]{0:T(128)}, u32[]{:S(2)}) copy-start(f32[128]{0:T(128)} %param.9) | copy-start | bytes 1540
  633.8 17.3 %copy-start.1 = (bf16[3,3,128,128]{3,2,1,0:T(8,128)(2,1)S(1)}, bf16[3,3,128,128]{3,2,1,0:T(8,128)(2,1)}, u32[]{:S(2)}) copy-start(bf16[3,3,128,128]{3,2,1,0:T(8,128)(2,1)} %param.6) | copy-start | bytes 884740
where the time goes:
time: 660 us; the launch traced here: 651 us
  blocking collectives  382 us (58%)
  local copies, waits for them, and re-layouts  128 us (19%)
  other arithmetic  48.5 us (7%)
  matrix products  47.1 us (7%)
  waiting for transfers between devices  23.2 us (4%)
  starting transfers between devices  21.7 us (3%)
    all_to_all x1, blocking collectives, body(): lax.all_to_all(step_one, 'row', split_axis=0, concat_axis=0, tiled=True)  189 us
    all_to_all x1, blocking collectives, body(): lax.all_to_all(blocks, 'col', split_axis=1, concat_axis=0, tiled=True)  96.8 us
    all_to_all x1, blocking collectives, body(): lax.all_to_all(step_two, 'col', split_axis=0, concat_axis=1, tiled=True)  96.6 us
    conv_general_dilated x2, matrix products, dilated(): lax.conv_general_dilated(source_map[None], kernel, (1, 1), 'VALID', rhs_d...  47.1 us
    conv_general_dilated x7, local copies, waits for them, and re-layouts, dilated(): lax.conv_general_dilated(source_map[None], kernel, (1, 1), 'VALID', rhs_d...  38.4 us
    convert_element_type x2, local copies, waits for them, and re-layouts, body(): mirrored.astype(jnp.float32)  26 us
    reshape x1, local copies, waits for them, and re-layouts, body(): blocks = blocks.reshape(block_count, tile_rows * tile_rows, channels)  24.6 us
    concatenate x2, other arithmetic, with_halo(): block = jnp.concatenate([low, block, high], axis=dim)  24 us
  transfers between devices with their start and end apart: 8, of which 8 were waited for; matrix products, arithmetic and copies ran while one was open for 0% of the time, Pallas kernels for 0%

commit v1 on v0

v1 whole, which is shorter than its diff:
```python
import functools

import jax
import jax.numpy as jnp
from jax import lax
from jax.experimental import pallas as pl
from jax.experimental.pallas import tpu as pltpu
from jax.sharding import PartitionSpec as P

REACH = 4
PAIR = 2 * REACH


def conv_kernel(steps, finish, first, odd, even, low, high, left, right, weights, offset, *rest):
    result, taps = rest[-2:]
    extra = rest[:-2]
    step = pl.program_id(0)
    cols = odd.shape[1]

    def widen(group, rows):
        slot = lax.rem(group + 4, 4)
        for r in range(REACH):
            line = rows[r]
            before = left[REACH * (group + 1) + r]
            after = right[REACH * (group + 1) + r]
            taps[slot, r] = jnp.concatenate(
                [
                    jnp.concatenate([before, line[: cols - REACH]], axis=0),
                    line,
                    jnp.concatenate([line[REACH:], after], axis=0),
                ],
                axis=1,
            )

    @pl.when(step == 0)
    def _():
        widen(-1, low)
        widen(0, first)

    widen(2 * step + 1, odd)

    @pl.when(step < steps - 1)
    def _():
        widen(2 * step + 2, even)

    @pl.when(step == steps - 1)
    def _():
        widen(2 * step + 2, high)

    slots = [lax.rem(2 * step + 3 + i, 4) for i in range(4)]
    for r in range(REACH):
        lines = jnp.concatenate([taps[slot, r] for slot in slots], axis=1)
        both = jnp.dot(lines, weights[...], preferred_element_type=jnp.float32)
        half = both.shape[1] // 2
        for i in range(2):
            value = both[:, half * i : half * (i + 1)] + offset[...]
            result[REACH * i + r] = finish(value, extra, REACH * i + r).astype(result.dtype)


def conv(block, low, high, left, right, kernel, offset, finish, extra=()):
    rows, cols, channels = block.shape
    steps = rows // PAIR
    taps = kernel.reshape(3, 3 * channels, channels)
    blank = jnp.zeros((3 * channels, channels), taps.dtype)
    weights = jnp.concatenate(
        [
            jnp.concatenate([taps[0], taps[1], taps[2], blank], axis=0),
            jnp.concatenate([blank, taps[0], taps[1], taps[2]], axis=0),
        ],
        axis=1,
    )
    four = (REACH, cols, channels)
    eight = pl.BlockSpec((PAIR, cols, channels), lambda g: (g, 0, 0))
    whole = pl.BlockSpec(memory_space=pltpu.VMEM)
    flops = 2 * rows * cols * channels * channels * 12
    moved = 2 * (2 + len(extra)) * rows * cols * channels
    return pl.pallas_call(
        functools.partial(conv_kernel, steps, finish),
        grid=(steps,),
        out_shape=jax.ShapeDtypeStruct(block.shape, jnp.bfloat16),
        in_specs=[
            pl.BlockSpec(four, lambda g: (0, 0, 0)),
            pl.BlockSpec(four, lambda g: (2 * g + 1, 0, 0)),
            pl.BlockSpec(four, lambda g: (jnp.minimum(2 * g + 2, 2 * steps - 1), 0, 0)),
            whole,
            whole,
            whole,
            whole,
            whole,
            whole,
        ]
        + [eight] * len(extra),
        out_specs=eight,
        scratch_shapes=[pltpu.VMEM((4, REACH, cols, 3 * channels), jnp.bfloat16)],
        compiler_params=pltpu.CompilerParams(vmem_limit_bytes=48 * 1024 * 1024),
        cost_estimate=pl.CostEstimate(flops=flops, bytes_accessed=moved, transcendentals=0),
    )(block, block, block, low, high, left, right, weights, offset.reshape(1, channels), *extra)


def finish_first(value, extra, r):
    return jnp.where(value > 0, value, jnp.exp(jnp.minimum(value, 0.0)) - 1.0)


def finish_second(value, extra, r):
    return value + extra[0][r].astype(jnp.float32)


def halos(block):
    def step(part, axis, up):
        count = lax.axis_size(axis)
        return lax.ppermute(
            part, axis, [(i, i + 1) if up else (i + 1, i) for i in range(count - 1)]
        )

    rows, cols = block.shape[:2]
    low = step(block[rows - REACH :], "row", True)
    high = step(block[:REACH], "row", False)
    ends = [
        jnp.concatenate([low[:, cut], block[:, cut], high[:, cut]], axis=0)
        for cut in (slice(cols - REACH, None), slice(0, REACH))
    ]
    return low, high, step(ends[0], "col", True), step(ends[1], "col", False)


def mirror_kernel(place, own, other, result):
    turned = jnp.swapaxes(other[...].astype(jnp.float32), 0, 1)
    result[...] = (0.5 * (own[...].astype(jnp.float32) + turned)).astype(result.dtype)


def symmetrize(own, other, place):
    rows, cols, channels = own.shape
    part = pl.BlockSpec((rows, rows, channels), lambda i, place: (0, place[0], 0))
    return pl.pallas_call(
        mirror_kernel,
        grid_spec=pltpu.PrefetchScalarGridSpec(
            num_scalar_prefetch=1,
            grid=(1,),
            in_specs=[part, pl.BlockSpec(other.shape, lambda i, place: (0, 0, 0))],
            out_specs=part,
        ),
        out_shape=jax.ShapeDtypeStruct(own.shape, own.dtype),
        input_output_aliases={1: 0},
        compiler_params=pltpu.CompilerParams(vmem_limit_bytes=48 * 1024 * 1024),
    )(place.reshape(1), own, other)


def exchange(own):
    rows, cols, channels = own.shape
    n_col = lax.axis_size("col")
    count = lax.axis_size("row") // n_col
    me = lax.rem(lax.axis_index("row"), count)

    def device(quarter, local, col):
        return (quarter * count + local % count) * n_col + col

    places = [(a, m, j) for a in range(n_col) for m in range(count) for j in range(n_col)]
    across = [(device(*p), device(p[0], p[1], n_col - 1 - p[2])) for p in places]
    landed = []
    for shift in range(count):
        block = lax.dynamic_slice_in_dim(own, lax.rem(me + shift, count) * rows, rows, 1)
        if shift % 2:
            pairs = [(device(a, m, j), device(j, m + shift, a)) for a, m, j in places]
        else:
            block = lax.ppermute(block, ("row", "col"), across)
            pairs = [
                (device(a, m, n_col - 1 - j), device(j, m + shift, a)) for a, m, j in places
            ]
        landed.append(lax.ppermute(block, ("row", "col"), pairs))
    result = own
    for shift in range(count):
        result = symmetrize(result, landed[shift], lax.rem(me - shift + count, count))
    return result


def body(activation, kernel_one, bias_one, kernel_two, bias_two):
    elu_out = conv(activation, *halos(activation), kernel_one, bias_one, finish_first)
    symmetric = exchange(elu_out)
    return conv(
        symmetric, *halos(symmetric), kernel_two, bias_two, finish_second, (symmetric,)
    )


def solution(mesh):
    in_specs = (P("row", "col", None), P(), P(), P(), P())
    out_specs = P("row", "col", None)
    return jax.shard_map(body, mesh=mesh, in_specs=in_specs, out_specs=out_specs, check_vma=False)
```

time: 660 us -> 354 us (0.54)
  blocking collectives: 382 us -> 0 us
  waiting for transfers between devices: 23.2 us -> 228 us
  local copies, waits for them, and re-layouts: 128 us -> 13.6 us
  Pallas kernels: 0 us -> 68.8 us
  matrix products: 47.1 us -> 0 us
  other arithmetic: 48.5 us -> 4.53 us
  starting transfers between devices: 21.7 us -> 35.1 us
    all_to_all x3 -> x0, blocking collectives: 382 us -> none  [the longest x1 189 us: body(): lax.all_to_all(step_one, 'row', split_axis=0, concat_axis=0, tiled=True)]
    ppermute x8 -> x20, waiting for transfers between devices: 23.2 us -> 228 us  [the longest x4 140 us: exchange(): block = lax.ppermute(block, ('row', 'col'), across)]
    pallas_call x0 -> x10, Pallas kernels: none -> 68.8 us  [the longest x2 43.5 us: conv(): pl.pallas_call(functools.partial(conv_kernel, steps, finish), grid=(steps...]
    conv_general_dilated x2 -> x0, matrix products: 47.1 us -> none  [dilated(): lax.conv_general_dilated(source_map[None], kernel, (1, 1), 'VALID', rhs_d...]
    conv_general_dilated x7 -> x0, local copies, waits for them, and re-layouts: 38.4 us -> none  [dilated(): lax.conv_general_dilated(source_map[None], kernel, (1, 1), 'VALID', rhs_d...]
    convert_element_type x3 -> x0, local copies, waits for them, and re-layouts: 38.2 us -> none  [the longest x2 26 us: body(): mirrored.astype(jnp.float32)]
    reshape x1 -> x0, local copies, waits for them, and re-layouts: 24.6 us -> none  [body(): blocks = blocks.reshape(block_count, tile_rows * tile_rows, channels)]
    convert_element_type x3 -> x0, other arithmetic: 23.5 us -> none  [the longest x1 11.3 us: body(): (0.5 * (elu_out.astype(jnp.float32) + mirrored.astype(jnp.float32))).asty...]
  transfers between devices with their start and end apart: 8 -> 20, of which waited for: 8 -> 13; matrix products, arithmetic and copies ran while one was open for 0% -> 2% of each run, Pallas kernels for 0% -> 6%
where the time goes in v1:
time: 354 us; the launch traced here: 351 us
  waiting for transfers between devices  228 us (64%)
  Pallas kernels  68.8 us (19%)
  starting transfers between devices  35.1 us (10%)
  local copies, waits for them, and re-layouts  13.6 us (4%)
  other arithmetic  4.53 us (1%)
    ppermute x4, waiting for transfers between devices, exchange(): block = lax.ppermute(block, ('row', 'col'), across)  140 us
    ppermute x8, waiting for transfers between devices, exchange(): landed.append(lax.ppermute(block, ('row', 'col'), pairs))  65.8 us
    pallas_call x2, Pallas kernels, conv(): pl.pallas_call(functools.partial(conv_kernel, steps, finish), grid=(steps...  43.5 us
    pallas_call x8, Pallas kernels, symmetrize(): pl.pallas_call(mirror_kernel, grid_spec=pltpu.PrefetchScalarGridSpec(num_...  25.2 us
    ppermute x8, starting transfers between devices, step(): lax.ppermute(part, axis, [(i, i + 1) if up else (i + 1, i) for i in range...  22.3 us
    ppermute x8, waiting for transfers between devices, step(): lax.ppermute(part, axis, [(i, i + 1) if up else (i + 1, i) for i in range...  22.2 us
    ppermute x8, starting transfers between devices, exchange(): landed.append(lax.ppermute(block, ('row', 'col'), pairs))  8.74 us
  transfers between devices with their start and end apart: 20, of which 13 were waited for; matrix products, arithmetic and copies ran while one was open for 2% of the time, Pallas kernels for 6%

profile of v1, /device:TPU:16, one launch (start us, length us, event | category | flops | bytes accessed | tf_op | source)
XLA Modules:
  0.0 350.6 jit_solution(1646647008280822197)
XLA Ops:
  1.3 2.8 collective-permute-start.1
  4.1 1.9 collective-permute-start
  7.2 3.7 %collective-permute-done.1.high = bf16[4,512,128]{2,1,0:T(8,128)(2,1)S(1)} collective-permute-done((bf16[4,512,128]{2,1,0:T(8,128)(2,1)S(1)}, bf16[4,512,128]{2,1,0:T(8,128)(2,1)S(1)}, u32[]{:S(2)}, u32[]{:S(2)}) %collective-permute-start.1) | collective-permute-done | bytes 524320 | tf_op jit(solution)/shard_map/ppermute | solution.py:111
  10.8 4.8 %collective-permute-done.low = bf16[4,512,128]{2,1,0:T(8,128)(2,1)S(1)} collective-permute-done((bf16[4,512,128]{2,1,0:T(8,128)(2,1)S(1)}, bf16[4,512,128]{2,1,0:T(8,128)(2,1)S(1)}, u32[]{:S(2)}, u32[]{:S(2)}) %collective-permute-start) | collective-permute-done | bytes 524320 | tf_op jit(solution)/shard_map/ppermute | solution.py:111
  15.7 3.4 collective-permute-start.2
  20.5 4.3 %fusion.1 = (bf16[1536,256]{1,0:T(8,128)(2,1)}, bf16[1536,256]{1,0:T(8,128)(2,1)S(1)}) fusion(bf16[384,128]{1,0:T(8,128)(2,1)S(1)} %broadcast.20, bf16[384,128]{1,0:T(8,128)(2,1)S(1)} %bitcast.22, bf16[384,128]{1,0:T(8,128)(2,1)S(1)} %bitcast.23, bf16[384,128]{1,0:T(8,128)(2,1)S(1)} %bitcast.21, bf16[384,128]{1,0:T(8,128)(2,1)S(1)} %bitcast.19, ...), kind=kLoop, calls=%fused_computation.5 | loop fusion | flops 11796480 | bytes 2260992 | tf_op jit(solution)/shard_map/concatenate | solution.py:65
  25.6 22.1 %shard_map.55.own = bf16[64,512,128]{2,1,0:T(8,128)(2,1)} custom-call(bf16[64,512,128]{2,1,0:T(8,128)(2,1)} %even.1, bf16[64,512,128]{2,1,0:T(8,128)(2,1)} %even.1, bf16[64,512,128]{2,1,0:T(8,128)(2,1)} %even.1, bf16[4,512,128]{2,1,0:T(8,128)(2,1)S(1)} %collective-permute-done.low, bf16[4,512,128]{2,1,0:T(8,128)(2,1)S(1)} %collective-permute-done.1.high, ...), custom_call_target="tpu_custom_call" | custom-call | flops 12884901888 | bytes 16777216 | tf_op jit(solution)/shard_map/pallas_call | solution.py:77
  47.7 6.6 %constant_dynamic-slice_fusion = (bf16[64,64,128]{2,1,0:T(8,128)(2,1)}, bf16[64,64,128]{2,1,0:T(8,128)(2,1)S(1)}, bf16[64,64,128]{2,1,0:T(8,128)(2,1)}, bf16[64,...) fusion(bf16[64,512,128]{2,1,0:T(8,128)(2,1)} %shard_map.55.own,, ...), kind=kLoop, calls=%fused_computation.14 | loop fusion | bytes 16777248 | tf_op jit(solution)/shard_map/dynamic_slice | solution.py:160
  54.3 1.9 collective-permute-start.7
  59.9 42.5 %collective-permute-done.7 = bf16[64,64,128]{2,1,0:T(8,128)(2,1)S(1)} collective-permute-done((bf16[64,64,128]{2,1,0:T(8,128)(2,1)S(1)}, bf16[64,64,128]{2,1,0:T(8,128)(2,1)S(1)}, u32[]{:S(2)}, u32[]{:S(2)}) %collective-permute-start.7) | collective-permute-done | bytes 1048608 | tf_op jit(solution)/shard_map/ppermute | solution.py:164
  102.4 3.5 collective-permute-start.8
  105.9 19.0 %collective-permute-done.4 = bf16[64,64,128]{2,1,0:T(8,128)(2,1)S(1)} collective-permute-done((bf16[64,64,128]{2,1,0:T(8,128)(2,1)S(1)}, bf16[64,64,128]{2,1,0:T(8,128)(2,1)S(1)}, u32[]{:S(2)}, u32[]{:S(2)}) %collective-permute-start.4) | collective-permute-done | bytes 1048608 | tf_op jit(solution)/shard_map/ppermute | solution.py:164
  124.8 33.4 %collective-permute-done.13 = bf16[64,64,128]{2,1,0:T(8,128)(2,1)} collective-permute-done((bf16[64,64,128]{2,1,0:T(8,128)(2,1)S(1)}, bf16[64,64,128]{2,1,0:T(8,128)(2,1)}, u32[]{:S(2)}, u32[]{:S(2)}) %collective-permute-start.13) | collective-permute-done | bytes 1048608 | tf_op jit(solution)/shard_map/ppermute | solution.py:164
  158.3 45.3 %collective-permute-done.10 = bf16[64,64,128]{2,1,0:T(8,128)(2,1)} collective-permute-done((bf16[64,64,128]{2,1,0:T(8,128)(2,1)S(1)}, bf16[64,64,128]{2,1,0:T(8,128)(2,1)}, u32[]{:S(2)}, u32[]{:S(2)}) %collective-permute-start.10) | collective-permute-done | bytes 1048608 | tf_op jit(solution)/shard_map/ppermute | solution.py:164
  204.7 3.7 %collective-permute-start.15 = (bf16[64,64,128]{2,1,0:T(8,128)(2,1)}, bf16[64,64,128]{2,1,0:T(8,128)(2,1)}, u32[]{:S(2)}, u32[]{:S(2)}) collective-permute-start(bf16[64,64,128]{2,1,0:T(8,128)(2,1)} %get-tuple-element.9), channel_id=1, source_target_pairs={{0,14},{1,30},{2,0},{3,16},{4,2},{5,18},{6,4},{7,20},{8,6},{9,22},... | collective-permute-start | bytes 3145736 | tf_op jit(solution)/shard_map/ppermute | solution.py:168
  209.6 3.0 shard_map.56.own
  212.6 3.0 shard_map.57.own
  215.6 3.0 shard_map.58.own
  218.6 3.0 shard_map.59.own
  221.6 21.9 %collective-permute-done.11.other = bf16[64,64,128]{2,1,0:T(8,128)(2,1)} collective-permute-done((bf16[64,64,128]{2,1,0:T(8,128)(2,1)}, bf16[64,64,128]{2,1,0:T(8,128)(2,1)}, u32[]{:S(2)}, u32[]{:S(2)}) %collective-permute-start.11) | collective-permute-done | bytes 1048608 | tf_op jit(solution)/shard_map/ppermute | solution.py:168
  243.5 3.3 shard_map.60.own
  246.8 3.3 shard_map.61.own
  250.0 43.9 %collective-permute-done.14.other = bf16[64,64,128]{2,1,0:T(8,128)(2,1)} collective-permute-done((bf16[64,64,128]{2,1,0:T(8,128)(2,1)}, bf16[64,64,128]{2,1,0:T(8,128)(2,1)}, u32[]{:S(2)}, u32[]{:S(2)}) %collective-permute-start.14) | collective-permute-done | bytes 1048608 | tf_op jit(solution)/shard_map/ppermute | solution.py:168
  294.0 3.3 shard_map.62.own
  297.3 3.3 shard_map.63.first.odd.even.rest_0_
  302.0 1.9 collective-permute-start.17
  303.9 2.4 collective-permute-start.16
  307.4 3.3 collective-permute-done.17.high
  310.7 4.8 %collective-permute-done.16.low = bf16[4,512,128]{2,1,0:T(8,128)(2,1)S(1)} collective-permute-done((bf16[4,512,128]{2,1,0:T(8,128)(2,1)S(1)}, bf16[4,512,128]{2,1,0:T(8,128)(2,1)S(1)}, u32[]{:S(2)}, u32[]{:S(2)}) %collective-permute-start.16) | collective-permute-done | bytes 524320 | tf_op jit(solution)/shard_map/ppermute | solution.py:111
  315.5 7.3 %collective-permute-start.18 = (bf16[72,4,128]{2,1,0:T(4,128)(2,1)S(1)}, bf16[72,4,128]{2,1,0:T(4,128)(2,1)S(1)}, u32[]{:S(2)}, u32[]{:S(2)}) collective-permute-start(bf16[72,4,128]{2,1,0:T(4,128)(2,1)S(1)} %pad_maximum_fusion.6), channel_id=1, source_target_pairs={{0,1},{2,3},{4,5},{6,7},{8,9},{10,11},{12,13},{14,15},{16,17},{18,... | collective-permute-start | bytes 221192 | tf_op jit(solution)/shard_map/ppermute | solution.py:111
  324.8 4.4 %collective-permute-done.19.right = bf16[72,4,128]{2,1,0:T(4,128)(2,1)S(1)} collective-permute-done((bf16[72,4,128]{2,1,0:T(4,128)(2,1)S(1)}, bf16[72,4,128]{2,1,0:T(4,128)(2,1)S(1)}, u32[]{:S(2)}, u32[]{:S(2)}) %collective-permute-start.19) | collective-permute-done | bytes 73760 | tf_op jit(solution)/shard_map/ppermute | solution.py:111
  329.1 21.4 %shard_map.64 = bf16[64,512,128]{2,1,0:T(8,128)(2,1)} custom-call(bf16[64,512,128]{2,1,0:T(8,128)(2,1)} %shard_map.63.first.odd.even.rest_0_, bf16[64,512,128]{2,1,0:T(8,128)(2,1)} %shard_map.63.first.odd.even.rest_0_, bf16[64,512,128]{2,1,0:T(8,128)(2,1)} %shard_map.63.first.odd.even.rest_0_, bf16[4,512,128]{2,1,0:T(8,128)(2,1)S(1)} %collective-permute-done.16.low, ...), custom_call_target="tpu_custom_call" | custom-call | flops 12884901888 | bytes 25165824 | tf_op jit(solution)/shard_map/pallas_call | solution.py:77
  (49 shorter events, 15.0 us)
Async XLA Ops:
  0.0 6.0 %copy-start.5 = (bf16[3,3,128,128]{3,2,1,0:T(8,128)(2,1)S(1)}, bf16[3,3,128,128]{3,2,1,0:T(8,128)(2,1)}, u32[]{:S(2)}) copy-start(bf16[3,3,128,128]{3,2,1,0:T(8,128)(2,1)} %param.6) | copy-start | bytes 884740
  0.0 7.1 %copy-start.6 = (bf16[3,3,128,128]{3,2,1,0:T(8,128)(2,1)S(1)}, bf16[3,3,128,128]{3,2,1,0:T(8,128)(2,1)}, u32[]{:S(2)}) copy-start(bf16[3,3,128,128]{3,2,1,0:T(8,128)(2,1)} %param.8) | copy-start | bytes 884740
  1.3 9.5 %collective-permute-start.1 = (bf16[4,512,128]{2,1,0:T(8,128)(2,1)S(1)}, bf16[4,512,128]{2,1,0:T(8,128)(2,1)S(1)}, u32[]{:S(2)}, u32[]{:S(2)}) collective-permute-start(bf16[4,512,128]{2,1,0:T(8,128)(2,1)S(1)} %get-tuple-element.19), channel_id=1, source_target_pairs={{2,0},{4,2},{6,4},{8,6},{10,8},{12,10},{14,12},{16,14},{18,16},{20... | collective-permute-start | bytes 1572872 | tf_op jit(solution)/shard_map/ppermute | solution.py:111
  4.1 11.5 %collective-permute-start = (bf16[4,512,128]{2,1,0:T(8,128)(2,1)S(1)}, bf16[4,512,128]{2,1,0:T(8,128)(2,1)S(1)}, u32[]{:S(2)}, u32[]{:S(2)}) collective-permute-start(bf16[4,512,128]{2,1,0:T(8,128)(2,1)S(1)} %get-tuple-element.20), channel_id=1, source_target_pairs={{0,2},{2,4},{4,6},{6,8},{8,10},{10,12},{12,14},{14,16},{16,18},{18... | collective-permute-start | bytes 1572872 | tf_op jit(solution)/shard_map/ppermute | solution.py:111
  7.1 18.4 %copy-start.3 = (f32[128]{0:T(128)S(1)}, f32[128]{0:T(128)}, u32[]{:S(2)}) copy-start(f32[128]{0:T(128)} %param.7) | copy-start | bytes 1540
  15.7 9.1 %collective-permute-start.2 = (bf16[72,4,128]{2,1,0:T(4,128)(2,1)S(1)}, bf16[72,4,128]{2,1,0:T(4,128)(2,1)S(1)}, u32[]{:S(2)}, u32[]{:S(2)}) collective-permute-start(bf16[72,4,128]{2,1,0:T(4,128)(2,1)S(1)} %pad_maximum_fusion.4), channel_id=1, source_target_pairs={{0,1},{2,3},{4,5},{6,7},{8,9},{10,11},{12,13},{14,15},{16,17},{18,... | collective-permute-start | bytes 221192 | tf_op jit(solution)/shard_map/ppermute | solution.py:111
  19.2 6.4 %collective-permute-start.3 = (bf16[72,4,128]{2,1,0:T(4,128)(2,1)S(1)}, bf16[72,4,128]{2,1,0:T(4,128)(2,1)S(1)}, u32[]{:S(2)}, u32[]{:S(2)}) collective-permute-start(bf16[72,4,128]{2,1,0:T(4,128)(2,1)S(1)} %pad_maximum_fusion.5), channel_id=1, source_target_pairs={{1,0},{3,2},{5,4},{7,6},{9,8},{11,10},{13,12},{15,14},{17,16},{19,... | collective-permute-start | bytes 221192 | tf_op jit(solution)/shard_map/ppermute | solution.py:111
  54.3 48.0 %collective-permute-start.7 = (bf16[64,64,128]{2,1,0:T(8,128)(2,1)S(1)}, bf16[64,64,128]{2,1,0:T(8,128)(2,1)S(1)}, u32[]{:S(2)}, u32[]{:S(2)}) collective-permute-start(bf16[64,64,128]{2,1,0:T(8,128)(2,1)S(1)} %get-tuple-element.14), channel_id=1, source_target_pairs={{0,1},{1,0},{2,3},{3,2},{4,5},{5,4},{6,7},{7,6},{8,9},{9,8},{10,11... | collective-permute-start | bytes 3145736 | tf_op jit(solution)/shard_map/ppermute | solution.py:164
  56.2 68.6 %collective-permute-start.4 = (bf16[64,64,128]{2,1,0:T(8,128)(2,1)S(1)}, bf16[64,64,128]{2,1,0:T(8,128)(2,1)S(1)}, u32[]{:S(2)}, u32[]{:S(2)}) collective-permute-start(bf16[64,64,128]{2,1,0:T(8,128)(2,1)S(1)} %get-tuple-element.16), channel_id=1, source_target_pairs={{0,1},{1,0},{2,3},{3,2},{4,5},{5,4},{6,7},{7,6},{8,9},{9,8},{10,11... | collective-permute-start | bytes 3145736 | tf_op jit(solution)/shard_map/ppermute | solution.py:164
  56.3 101.9 %collective-permute-start.13 = (bf16[64,64,128]{2,1,0:T(8,128)(2,1)S(1)}, bf16[64,64,128]{2,1,0:T(8,128)(2,1)}, u32[]{:S(2)}, u32[]{:S(2)}) collective-permute-start(bf16[64,64,128]{2,1,0:T(8,128)(2,1)S(1)} %get-tuple-element.10), channel_id=1, source_target_pairs={{0,1},{1,0},{2,3},{3,2},{4,5},{5,4},{6,7},{7,6},{8,9},{9,8},{10,11... | collective-permute-start | bytes 3145736 | tf_op jit(solution)/shard_map/ppermute | solution.py:164
  58.2 145.4 %collective-permute-start.10 = (bf16[64,64,128]{2,1,0:T(8,128)(2,1)S(1)}, bf16[64,64,128]{2,1,0:T(8,128)(2,1)}, u32[]{:S(2)}, u32[]{:S(2)}) collective-permute-start(bf16[64,64,128]{2,1,0:T(8,128)(2,1)S(1)} %get-tuple-element.12), channel_id=1, source_target_pairs={{0,1},{1,0},{2,3},{3,2},{4,5},{5,4},{6,7},{7,6},{8,9},{9,8},{10,11... | collective-permute-start | bytes 3145736 | tf_op jit(solution)/shard_map/ppermute | solution.py:164
  58.4 145.2 %collective-permute-start.6 = (bf16[64,64,128]{2,1,0:T(8,128)(2,1)S(1)}, bf16[64,64,128]{2,1,0:T(8,128)(2,1)S(1)}, u32[]{:S(2)}, u32[]{:S(2)}) collective-permute-start(bf16[64,64,128]{2,1,0:T(8,128)(2,1)S(1)} %get-tuple-element.15), channel_id=1, source_target_pairs={{0,2},{1,18},{2,4},{3,20},{4,6},{5,22},{6,8},{7,24},{8,10},{9,26},... | collective-permute-start | bytes 3145736 | tf_op jit(solution)/shard_map/ppermute | solution.py:168
  102.4 101.2 %collective-permute-start.8 = (bf16[64,64,128]{2,1,0:T(8,128)(2,1)S(1)}, bf16[64,64,128]{2,1,0:T(8,128)(2,1)S(1)}, u32[]{:S(2)}, u32[]{:S(2)}) collective-permute-start(bf16[64,64,128]{2,1,0:T(8,128)(2,1)S(1)} %collective-permute-done.7), channel_id=1, source_target_pairs={{1,4},{0,20},{3,6},{2,22},{5,8},{4,24},{7,10},{6,26},{9,12},{8,28}... | collective-permute-start | bytes 3145736 | tf_op jit(solution)/shard_map/ppermute | solution.py:168
  124.8 78.8 %collective-permute-start.5 = (bf16[64,64,128]{2,1,0:T(8,128)(2,1)S(1)}, bf16[64,64,128]{2,1,0:T(8,128)(2,1)S(1)}, u32[]{:S(2)}, u32[]{:S(2)}) collective-permute-start(bf16[64,64,128]{2,1,0:T(8,128)(2,1)S(1)} %collective-permute-done.4), channel_id=1, source_target_pairs={{1,0},{0,16},{3,2},{2,18},{5,4},{4,20},{7,6},{6,22},{9,8},{8,24},{... | collective-permute-start | bytes 3145736 | tf_op jit(solution)/shard_map/ppermute | solution.py:168
  158.3 60.3 %collective-permute-start.9 = (bf16[64,64,128]{2,1,0:T(8,128)(2,1)}, bf16[64,64,128]{2,1,0:T(8,128)(2,1)S(1)}, u32[]{:S(2)}, u32[]{:S(2)}) collective-permute-start(bf16[64,64,128]{2,1,0:T(8,128)(2,1)} %get-tuple-element.13), channel_id=1, source_target_pairs={{0,6},{1,22},{2,8},{3,24},{4,10},{5,26},{6,12},{7,28},{8,14},{9,30... | collective-permute-start | bytes 3145736 | tf_op jit(solution)/shard_map/ppermute | solution.py:168
  203.6 39.9 %collective-permute-start.11 = (bf16[64,64,128]{2,1,0:T(8,128)(2,1)}, bf16[64,64,128]{2,1,0:T(8,128)(2,1)}, u32[]{:S(2)}, u32[]{:S(2)}) collective-permute-start(bf16[64,64,128]{2,1,0:T(8,128)(2,1)} %collective-permute-done.10), channel_id=1, source_target_pairs={{1,8},{0,24},{3,10},{2,26},{5,12},{4,28},{7,14},{6,30},{9,0},{8,16... | collective-permute-start | bytes 3145736 | tf_op jit(solution)/shard_map/ppermute | solution.py:168
  203.6 43.2 %collective-permute-start.12 = (bf16[64,64,128]{2,1,0:T(8,128)(2,1)}, bf16[64,64,128]{2,1,0:T(8,128)(2,1)}, u32[]{:S(2)}, u32[]{:S(2)}) collective-permute-start(bf16[64,64,128]{2,1,0:T(8,128)(2,1)} %get-tuple-element.11), channel_id=1, source_target_pairs={{0,10},{1,26},{2,12},{3,28},{4,14},{5,30},{6,0},{7,16},{8,2},{9,18... | collective-permute-start | bytes 3145736 | tf_op jit(solution)/shard_map/ppermute | solution.py:168
  203.6 90.3 %collective-permute-start.14 = (bf16[64,64,128]{2,1,0:T(8,128)(2,1)}, bf16[64,64,128]{2,1,0:T(8,128)(2,1)}, u32[]{:S(2)}, u32[]{:S(2)}) collective-permute-start(bf16[64,64,128]{2,1,0:T(8,128)(2,1)} %collective-permute-done.13), channel_id=1, source_target_pairs={{1,12},{0,28},{3,14},{2,30},{5,0},{4,16},{7,2},{6,18},{9,4},{8,20}... | collective-permute-start | bytes 3145736 | tf_op jit(solution)/shard_map/ppermute | solution.py:168
  203.7 1.0 copy-start
  204.7 92.6 %collective-permute-start.15 = (bf16[64,64,128]{2,1,0:T(8,128)(2,1)}, bf16[64,64,128]{2,1,0:T(8,128)(2,1)}, u32[]{:S(2)}, u32[]{:S(2)}) collective-permute-start(bf16[64,64,128]{2,1,0:T(8,128)(2,1)} %get-tuple-element.9), channel_id=1, source_target_pairs={{0,14},{1,30},{2,0},{3,16},{4,2},{5,18},{6,4},{7,20},{8,6},{9,22},... | collective-permute-start | bytes 3145736 | tf_op jit(solution)/shard_map/ppermute | solution.py:168
  208.3 1.2 copy-start.1
  300.6 28.5 %copy-start.2 = (bf16[1536,256]{1,0:T(8,128)(2,1)S(1)}, bf16[1536,256]{1,0:T(8,128)(2,1)}, u32[]{:S(2)}) copy-start(bf16[1536,256]{1,0:T(8,128)(2,1)} %get-tuple-element.35.weights) | copy-start | bytes 2359300
  300.6 28.5 %copy-start.4 = (f32[128]{0:T(128)S(1)}, f32[128]{0:T(128)}, u32[]{:S(2)}) copy-start(f32[128]{0:T(128)} %param.9) | copy-start | bytes 1540
  302.0 8.6 %collective-permute-start.17 = (bf16[4,512,128]{2,1,0:T(8,128)(2,1)S(1)}, bf16[4,512,128]{2,1,0:T(8,128)(2,1)S(1)}, u32[]{:S(2)}, u32[]{:S(2)}) collective-permute-start(bf16[4,512,128]{2,1,0:T(8,128)(2,1)S(1)} %get-tuple-element.7), channel_id=1, source_target_pairs={{2,0},{4,2},{6,4},{8,6},{10,8},{12,10},{14,12},{16,14},{18,16},{20... | collective-permute-start | bytes 1572872 | tf_op jit(solution)/shard_map/ppermute | solution.py:111
  303.9 11.5 %collective-permute-start.16 = (bf16[4,512,128]{2,1,0:T(8,128)(2,1)S(1)}, bf16[4,512,128]{2,1,0:T(8,128)(2,1)S(1)}, u32[]{:S(2)}, u32[]{:S(2)}) collective-permute-start(bf16[4,512,128]{2,1,0:T(8,128)(2,1)S(1)} %get-tuple-element.8), channel_id=1, source_target_pairs={{0,2},{2,4},{4,6},{6,8},{8,10},{10,12},{12,14},{14,16},{16,18},{18... | collective-permute-start | bytes 1572872 | tf_op jit(solution)/shard_map/ppermute | solution.py:111
  315.5 9.3 %collective-permute-start.18 = (bf16[72,4,128]{2,1,0:T(4,128)(2,1)S(1)}, bf16[72,4,128]{2,1,0:T(4,128)(2,1)S(1)}, u32[]{:S(2)}, u32[]{:S(2)}) collective-permute-start(bf16[72,4,128]{2,1,0:T(4,128)(2,1)S(1)} %pad_maximum_fusion.6), channel_id=1, source_target_pairs={{0,1},{2,3},{4,5},{6,7},{8,9},{10,11},{12,13},{14,15},{16,17},{18,... | collective-permute-start | bytes 221192 | tf_op jit(solution)/shard_map/ppermute | solution.py:111
  322.9 6.2 %collective-permute-start.19 = (bf16[72,4,128]{2,1,0:T(4,128)(2,1)S(1)}, bf16[72,4,128]{2,1,0:T(4,128)(2,1)S(1)}, u32[]{:S(2)}, u32[]{:S(2)}) collective-permute-start(bf16[72,4,128]{2,1,0:T(4,128)(2,1)S(1)} %pad_maximum_fusion.7), channel_id=1, source_target_pairs={{1,0},{3,2},{5,4},{7,6},{9,8},{11,10},{13,12},{15,14},{17,16},{19,... | collective-permute-start | bytes 221192 | tf_op jit(solution)/shard_map/ppermute | solution.py:111

commit v2 on v0

v2 whole, which is shorter than its diff:
```python
import functools

import jax
import jax.numpy as jnp
from jax import lax
from jax.experimental import pallas as pl
from jax.experimental.pallas import tpu as pltpu
from jax.sharding import PartitionSpec as P

REACH = 4
PAIR = 2 * REACH
ROOM = pltpu.CompilerParams(vmem_limit_bytes=48 * 1024 * 1024)


def widen(taps, slot, rows, before, after):
    cols = rows.shape[1]
    for r in range(REACH):
        line = rows[r]
        taps[slot, r] = jnp.concatenate(
            [
                jnp.concatenate([before[r], line[: cols - REACH]], axis=0),
                line,
                jnp.concatenate([line[REACH:], after[r]], axis=0),
            ],
            axis=1,
        )


def multiply(taps, slots, weights, offset, finish):
    for r in range(REACH):
        lines = jnp.concatenate([taps[slot, r] for slot in slots], axis=1)
        both = jnp.dot(lines, weights[...], preferred_element_type=jnp.float32)
        half = both.shape[1] // 2
        for i in range(2):
            finish(both[:, half * i : half * (i + 1)] + offset[...], REACH * i + r)


def inner_kernel(finish, me, one, two, odd, even, left, right, weights, offset, *rest):
    taps = rest[-1]
    step = pl.program_id(0) + 1

    def fill(group, rows):
        at = pl.ds(REACH * group, REACH)
        widen(taps, lax.rem(group, 4), rows, left[at], right[at])

    @pl.when(step == 1)
    def _():
        fill(1, one)
        fill(2, two)

    fill(2 * step + 1, odd)
    fill(2 * step + 2, even)
    slots = [lax.rem(2 * step + 3 + i, 4) for i in range(4)]
    multiply(taps, slots, weights, offset, functools.partial(finish, me, rest))


def outer_kernel(finish, me, low, high, one, two, three, left, right, weights, offset, *rest):
    taps = rest[-1]
    end = pl.program_id(0)
    cols = one.shape[1]

    def fill(slot, rows):
        at = pl.ds(REACH * slot, REACH)
        widen(taps, slot, rows, left[0, at], right[0, at])

    @pl.when(end == 0)
    def _():
        fill(0, low[:, :cols])

    @pl.when(end == 1)
    def _():
        fill(3, high[:, :cols])

    for i, rows in enumerate((one, two, three)):
        fill(i + 1 - end, rows)
    multiply(taps, range(4), weights, offset, functools.partial(finish, me, rest))


def paired(kernel):
    channels = kernel.shape[-1]
    taps = kernel.reshape(3, 3 * channels, channels)
    blank = jnp.zeros((1, 3 * channels, channels), taps.dtype)
    halves = [jnp.concatenate([taps, blank]), jnp.concatenate([blank, taps])]
    return jnp.concatenate([h.reshape(12 * channels, channels) for h in halves], axis=1)


def conv(block, halos, kernel, offset, finish, shapes, me, extra=(), scratch=()):
    rows, cols, channels = block.shape
    steps, groups = rows // PAIR, rows // REACH
    weights, offset = paired(kernel), offset.reshape(1, channels)
    (left, right), (low, high, left_ends, right_ends) = halos
    four = (REACH, cols, channels)
    whole = pl.BlockSpec(memory_space=pltpu.VMEM)
    scratch = [*scratch, pltpu.VMEM((4, REACH, cols, 3 * channels), jnp.bfloat16)]
    outs = [jax.ShapeDtypeStruct(s, jnp.bfloat16) for s in shapes]

    def slab(shape, step_of):
        size = (*shape[:-3], PAIR, *shape[-2:])
        lead = (0,) * (len(shape) - 3)
        return pl.BlockSpec(size, lambda g, me: (*lead, step_of(g), 0, 0))

    def cost(count):
        work = count * PAIR * cols * channels
        return pl.CostEstimate(
            flops=24 * work * channels, bytes_accessed=8 * work, transcendentals=0
        )

    inner = lambda g: g + 1
    results = pl.pallas_call(
        functools.partial(inner_kernel, finish),
        grid_spec=pltpu.PrefetchScalarGridSpec(
            num_scalar_prefetch=1,
            grid=(steps - 2,),
            in_specs=[
                pl.BlockSpec(four, lambda g, me: (1, 0, 0)),
                pl.BlockSpec(four, lambda g, me: (2, 0, 0)),
                pl.BlockSpec(four, lambda g, me: (2 * g + 3, 0, 0)),
                pl.BlockSpec(four, lambda g, me: (2 * g + 4, 0, 0)),
            ]
            + [whole] * 4
            + [slab(e.shape, inner) for e in extra],
            out_specs=[slab(s, inner) for s in shapes],
            scratch_shapes=scratch,
        ),
        out_shape=outs,
        compiler_params=ROOM,
        cost_estimate=cost(steps - 2),
    )(me, block, block, block, block, left, right, weights, offset, *extra)

    def third(i):
        return pl.BlockSpec(four, lambda e, me: (i + e * (groups - 3), 0, 0))

    def at_end(array):
        return pl.BlockSpec((1, *array.shape[1:]), lambda e, me: (e, 0, 0, 0))

    outer = lambda e: e * (steps - 1)
    given = [me, low, high, block, block, block, left_ends, right_ends, weights, offset, *extra]
    return pl.pallas_call(
        functools.partial(outer_kernel, finish),
        grid_spec=pltpu.PrefetchScalarGridSpec(
            num_scalar_prefetch=1,
            grid=(2,),
            in_specs=[whole, whole, third(0), third(1), third(2)]
            + [at_end(left_ends), at_end(right_ends), whole, whole]
            + [slab(e.shape, outer) for e in extra]
            + [pl.BlockSpec(memory_space=pl.ANY)] * len(outs),
            out_specs=[slab(s, outer) for s in shapes],
            scratch_shapes=scratch,
        ),
        out_shape=outs,
        input_output_aliases={len(given) + i: i for i in range(len(outs))},
        compiler_params=ROOM,
        cost_estimate=cost(2),
    )(*given, *results)


def finish_first(count, groups, me, rest, value, r):
    line, outs = rest[-2], rest[-2 - len(groups) : -2]
    value = jnp.where(value > 0, value, jnp.exp(jnp.minimum(value, 0.0)) - 1.0)
    line[...] = value
    size = outs[0].shape[-2]
    for out, group in zip(outs, groups):
        for n, shift in enumerate(group):
            start = pl.multiple_of(lax.rem(me[0] + shift, count) * size, size)
            out[n, r] = line[pl.ds(start, size)].astype(out.dtype)


def finish_second(me, rest, value, r):
    own, result = rest[0], rest[-2]
    result[r] = (value + own[r].astype(jnp.float32)).astype(result.dtype)


def halos(block):
    def move(part, axis, up):
        count = lax.axis_size(axis)
        return lax.ppermute(
            part, axis, [(i, i + 1) if up else (i + 1, i) for i in range(count - 1)]
        )

    rows, cols = block.shape[:2]
    if lax.axis_size("col") == 2:
        first = lax.axis_index("col") == 0
        edge = jnp.where(first, block[:, cols - REACH :], block[:, :REACH])
        edge = lax.ppermute(edge, "col", [(0, 1), (1, 0)])
        left, right = jnp.where(first, 0, edge), jnp.where(first, edge, 0)
    else:
        left = move(block[:, cols - REACH :], "col", True)
        right = move(block[:, :REACH], "col", False)
    wide = [
        jnp.concatenate([array[cut] for array in (block, left, right)], axis=1)
        for cut in (slice(rows - REACH, None), slice(0, REACH))
    ]
    low, high = move(wide[0], "row", True), move(wide[1], "row", False)
    reach = 3 * REACH
    ends = [
        jnp.stack(
            [
                jnp.concatenate([low[:, at : at + REACH], side[:reach]]),
                jnp.concatenate([side[rows - reach :], high[:, at : at + REACH]]),
            ]
        )
        for at, side in ((cols, left), (cols + REACH, right))
    ]
    return (left, right), (low, high, *ends)


def mirror_kernel(sizes, place, own, *rest):
    result = rest[-1]
    parts = iter(rest)
    start = 0
    for size, choice in sizes:
        other = next(parts)[...].astype(jnp.float32)
        if choice:
            mine = next(parts)[...].astype(jnp.float32)
            other = jnp.where(place[1] == 1, mine, other)
        cut = slice(start, start + size)
        turned = jnp.swapaxes(other, 0, 1)
        value = 0.5 * (own[0, :, cut].astype(jnp.float32) + turned)
        result[:, cut] = value.astype(result.dtype)
        start += size


def symmetrize(so_far, shape, own, index, parts, place):
    rows, channels = own.shape[1], own.shape[3]
    arrays = [array for part in parts for array in part]
    sizes = [(part[0].shape[0], len(part) > 1) for part in parts]
    out = pl.BlockSpec((rows, rows, channels), lambda i, place: (0, place[0], 0))
    given = [place, own, *arrays]
    first = so_far is None
    return pl.pallas_call(
        functools.partial(mirror_kernel, sizes),
        grid_spec=pltpu.PrefetchScalarGridSpec(
            num_scalar_prefetch=1,
            grid=(1,),
            in_specs=[pl.BlockSpec((1, rows, rows, channels), lambda i, place: (index, 0, 0, 0))]
            + [pl.BlockSpec(a.shape, lambda i, place: (0, 0, 0)) for a in arrays]
            + [pl.BlockSpec(memory_space=pl.ANY)] * (not first),
            out_specs=out,
        ),
        out_shape=jax.ShapeDtypeStruct(shape, own.dtype),
        input_output_aliases={} if first else {len(given): 0},
        compiler_params=ROOM,
    )(*given, *([] if first else [so_far]))


def groups_of(n_col, count):
    if n_col != 2 or count < 4:
        return [(s,) for s in range(count)]
    return [(s,) for s in range(count)]


def exchange(pieces, shape, me):
    n_col = lax.axis_size("col")
    count = lax.axis_size("row") // n_col
    rows, channels = shape[0], shape[2]
    mine = (lax.axis_index("row") // count == lax.axis_index("col")).astype(jnp.int32)
    groups = groups_of(n_col, count)
    where = {s: (i, n) for i, group in enumerate(groups) for n, s in enumerate(group)}

    def device(quarter, local, col):
        return (quarter * count + local % count) * n_col + col

    places = [(a, m, j) for a in range(n_col) for m in range(count) for j in range(n_col)]

    def send(block, pairs):
        return lax.ppermute(block, ("row", "col"), pairs)

    def direct(block, shift):
        return send(block, [(device(*p), device(p[2], p[1] + shift, p[0])) for p in places])

    def piece(shift):
        i, n = where[shift]
        return pieces[i][n]

    landed = {}
    if n_col != 2:
        for s in range(count):
            landed[s] = [(direct(piece(s), s),)]
    else:
        across = [(device(*p), device(p[0], p[1], 1 - p[2])) for p in places]
        for s in range(count):
            if s % 2:
                landed[s] = [(direct(piece(s), s),)]
            else:
                hop = send(piece(s), across)
                pairs = [(device(a, m, 1 - j), device(j, m + s, a)) for a, m, j in places]
                landed[s] = [(send(hop, pairs),)]
    result = None
    for s in [s for s in range(count) if s in landed] + [s for s in landed if s > 7]:
        i, n = where[-s % count]
        place = jnp.stack([lax.rem(me[0] - s + count, count), mine])
        result = symmetrize(result, shape, pieces[i], n, landed[s], place)
    return result


def body(activation, kernel_one, bias_one, kernel_two, bias_two):
    rows, cols, channels = activation.shape
    n_col = lax.axis_size("col")
    count = lax.axis_size("row") // n_col
    me = lax.rem(lax.axis_index("row"), count).astype(jnp.int32).reshape(1)
    groups = groups_of(n_col, count)
    shapes = [(len(g), rows, rows, channels) for g in groups]
    pieces = conv(
        activation,
        halos(activation),
        kernel_one,
        bias_one,
        functools.partial(finish_first, count, groups),
        shapes,
        me,
        scratch=(pltpu.VMEM((cols, channels), jnp.float32),),
    )
    symmetric = exchange(pieces, activation.shape, me)
    return conv(
        symmetric,
        halos(symmetric),
        kernel_two,
        bias_two,
        finish_second,
        [activation.shape],
        me,
        extra=(symmetric,),
    )[0]


def solution(mesh):
    in_specs = (P("row", "col", None), P(), P(), P(), P())
    out_specs = P("row", "col", None)
    return jax.shard_map(body, mesh=mesh, in_specs=in_specs, out_specs=out_specs, check_vma=False)
```

time: 660 us -> 340 us (0.52); the launches traced: 651 us -> 340 us
  blocking collectives: 382 us -> 0 us
  waiting for transfers between devices: 23.2 us -> 197 us
  local copies, waits for them, and re-layouts: 128 us -> 5.61 us
  Pallas kernels: 0 us -> 83.5 us
  matrix products: 47.1 us -> 0 us
  other arithmetic: 48.5 us -> 5.27 us
  starting transfers between devices: 21.7 us -> 48.2 us
    all_to_all x3 -> x0, blocking collectives: 382 us -> none  [the longest x1 189 us: body(): lax.all_to_all(step_one, 'row', split_axis=0, concat_axis=0, tiled=True)]
    ppermute x8 -> x18, waiting for transfers between devices: 23.2 us -> 197 us  [the longest x12 194 us: send(): return lax.ppermute(block, ('row', 'col'), pairs)]
    pallas_call x0 -> x12, Pallas kernels: none -> 83.5 us  [the longest x2 37.5 us: conv(): pl.pallas_call(functools.partial(inner_kernel, finish), grid_spec=pltpu.P...]
    conv_general_dilated x2 -> x0, matrix products: 47.1 us -> none  [dilated(): lax.conv_general_dilated(source_map[None], kernel, (1, 1), 'VALID', rhs_d...]
    conv_general_dilated x7 -> x0, local copies, waits for them, and re-layouts: 38.4 us -> none  [dilated(): lax.conv_general_dilated(source_map[None], kernel, (1, 1), 'VALID', rhs_d...]
    convert_element_type x3 -> x0, local copies, waits for them, and re-layouts: 38.2 us -> none  [the longest x2 26 us: body(): mirrored.astype(jnp.float32)]
    ppermute x8 -> x18, starting transfers between devices: 21.7 us -> 48.2 us  [the longest x12 35.4 us: send(): return lax.ppermute(block, ('row', 'col'), pairs)]
    reshape x1 -> x0, local copies, waits for them, and re-layouts: 24.6 us -> none  [body(): blocks = blocks.reshape(block_count, tile_rows * tile_rows, channels)]
  transfers between devices with their start and end apart: 8 -> 18, of which waited for: 8 -> 7; matrix products, arithmetic and copies ran while one was open for 0% -> 2% of each run, Pallas kernels for 0% -> 18%
where the time goes in v2:
time: 340 us
  waiting for transfers between devices  197 us (58%)
  Pallas kernels  83.5 us (25%)
  starting transfers between devices  48.2 us (14%)
  local copies, waits for them, and re-layouts  5.61 us (2%)
  other arithmetic  5.27 us (2%)
    ppermute x12, waiting for transfers between devices, send(): return lax.ppermute(block, ('row', 'col'), pairs)  194 us
    pallas_call x2, Pallas kernels, conv(): pl.pallas_call(functools.partial(inner_kernel, finish), grid_spec=pltpu.P...  37.5 us
    ppermute x12, starting transfers between devices, send(): return lax.ppermute(block, ('row', 'col'), pairs)  35.4 us
    pallas_call x8, Pallas kernels, symmetrize(): pl.pallas_call(functools.partial(mirror_kernel, sizes), grid_spec=pltpu.P...  28.3 us
    pallas_call x2, Pallas kernels, conv(): pl.pallas_call(functools.partial(outer_kernel, finish), grid_spec=pltpu.P...  17.7 us
    ppermute x4, starting transfers between devices, move(): lax.ppermute(part, axis, [(i, i + 1) if up else (i + 1, i) for i in range...  11.2 us
  transfers between devices with their start and end apart: 18, of which 7 were waited for; matrix products, arithmetic and copies ran while one was open for 2% of the time, Pallas kernels for 18%

profile of v2, /device:TPU:16, one launch (start us, length us, event | category | flops | bytes accessed | tf_op | source)
XLA Modules:
  0.0 339.9 jit_solution(17005545610287917715)
XLA Ops:
  1.1 1.6 collective-permute-start
  2.7 1.3 fusion.1
  6.0 2.6 collective-permute-start.2
  8.7 1.9 collective-permute-start.1
  10.6 19.5 %shard_map.55 = (bf16[1,64,64,128]{3,2,1,0:T(8,128)(2,1)S(1)}, bf16[1,64,64,128]{3,2,1,0:T(8,128)(2,1)S(1)}, bf16[1,64,64,128]{3,2,1,0:T(8,128)(2,1)S(1)}, bf16[...) custom-call(s32[1]{0:T(128)} %bitcast.me, ...), custom_call_target="tpu_custom_call" | custom-call | flops 9663676416 | bytes 25165824 | tf_op jit(solution)/shard_map/pallas_call | solution.py:109
  31.3 8.7 %shard_map.56 = (bf16[1,64,64,128]{3,2,1,0:T(8,128)(2,1)S(1)}, bf16[1,64,64,128]{3,2,1,0:T(8,128)(2,1)S(1)}, bf16[1,64,64,128]{3,2,1,0:T(8,128)(2,1)S(1)}, bf16[...) custom-call(s32[1]{0:T(128)} %bitcast.me, ...), custom_call_target="tpu_custom_call", output_to_operand_aliasing={{0}: (10, {}), {1}: (11, {}), {2}: (12, {}), {3}: (13, {}),... | custom-call | flops 3221225472 | bytes 8388608 | tf_op jit(solution)/shard_map/pallas_call | solution.py:138
  41.8 1.2 collective-permute-start.10
  44.4 1.4 collective-permute-start.4
  45.8 43.7 %collective-permute-done.13 = bf16[64,64,128]{2,1,0:T(8,128)(2,1)} collective-permute-done((bf16[64,64,128]{2,1,0:T(8,128)(2,1)S(1)}, bf16[64,64,128]{2,1,0:T(8,128)(2,1)}, u32[]{:S(2)}, u32[]{:S(2)}) %collective-permute-start.13) | collective-permute-done | bytes 1048608 | tf_op jit(solution)/shard_map/ppermute | solution.py:266
  89.5 22.5 %collective-permute-done.10 = bf16[64,64,128]{2,1,0:T(8,128)(2,1)} collective-permute-done((bf16[64,64,128]{2,1,0:T(8,128)(2,1)S(1)}, bf16[64,64,128]{2,1,0:T(8,128)(2,1)}, u32[]{:S(2)}, u32[]{:S(2)}) %collective-permute-start.10) | collective-permute-done | bytes 1048608 | tf_op jit(solution)/shard_map/ppermute | solution.py:266
  112.0 1.7 collective-permute-start.9
  113.6 39.1 %collective-permute-done.7 = bf16[64,64,128]{2,1,0:T(8,128)(2,1)} collective-permute-done((bf16[64,64,128]{2,1,0:T(8,128)(2,1)}, bf16[64,64,128]{2,1,0:T(8,128)(2,1)}, u32[]{:S(2)}, u32[]{:S(2)}) %collective-permute-start.7) | collective-permute-done | bytes 1048608 | tf_op jit(solution)/shard_map/ppermute | solution.py:266
  152.9 22.3 %collective-permute-done.4 = bf16[64,64,128]{2,1,0:T(8,128)(2,1)} collective-permute-done((bf16[64,64,128]{2,1,0:T(8,128)(2,1)}, bf16[64,64,128]{2,1,0:T(8,128)(2,1)}, u32[]{:S(2)}, u32[]{:S(2)}) %collective-permute-start.4) | collective-permute-done | bytes 1048608 | tf_op jit(solution)/shard_map/ppermute | solution.py:266
  175.2 23.6 %collective-permute-start.3 = (bf16[64,64,128]{2,1,0:T(8,128)(2,1)}, bf16[64,64,128]{2,1,0:T(8,128)(2,1)}, u32[]{:S(2)}, u32[]{:S(2)}) collective-permute-start(bf16[64,64,128]{2,1,0:T(8,128)(2,1)} %bitcast.49), channel_id=1, source_target_pairs={{0,14},{1,30},{2,0},{3,16},{4,2},{5,18},{6,4},{7,20},{8,6},{9,22},... | collective-permute-start | bytes 3145736 | tf_op jit(solution)/shard_map/ppermute | solution.py:266
  198.8 3.6 %collective-permute-start.8 = (bf16[64,64,128]{2,1,0:T(8,128)(2,1)}, bf16[64,64,128]{2,1,0:T(8,128)(2,1)}, u32[]{:S(2)}, u32[]{:S(2)}) collective-permute-start(bf16[64,64,128]{2,1,0:T(8,128)(2,1)} %collective-permute-done.7), channel_id=1, source_target_pairs={{1,8},{0,24},{3,10},{2,26},{5,12},{4,28},{7,14},{6,30},{9,0},{8,16... | collective-permute-start | bytes 3145736 | tf_op jit(solution)/shard_map/ppermute | solution.py:266
  202.4 1.5 collective-permute-start.5
  205.6 3.5 %shard_map.57.rest_1_ = bf16[64,512,128]{2,1,0:T(8,128)(2,1)} custom-call(s32[2]{0:T(128)S(1)} %pad_add_fusion.7.place, bf16[1,64,64,128]{3,2,1,0:T(8,128)(2,1)S(1)} %get-tuple-element.36.own, bf16[64,64,128]{2,1,0:T(8,128)(2,1)} %collective-permute-done.14.rest_0_), custom_call_target="tpu_custom_call" | custom-call | tf_op jit(solution)/shard_map/pallas_call | solution.py:230
  209.2 3.6 %shard_map.58.rest_1_ = bf16[64,512,128]{2,1,0:T(8,128)(2,1)} custom-call(s32[2]{0:T(128)S(1)} %pad_add_fusion.6.place, bf16[1,64,64,128]{3,2,1,0:T(8,128)(2,1)S(1)} %copy-done.6, bf16[64,64,128]{2,1,0:T(8,128)(2,1)} %collective-permute-done.12.rest_0_, bf16[64,512,128]{2,1,0:T(8,128)(2,1)} %shard_map.57.rest_1_), custom_call_target="tpu_custom_call", output_to_operand_aliasing={{}: (3, {})} | custom-call | tf_op jit(solution)/shard_map/pallas_call | solution.py:230
  212.8 3.5 %shard_map.59.rest_1_ = bf16[64,512,128]{2,1,0:T(8,128)(2,1)} custom-call(s32[2]{0:T(128)S(1)} %pad_add_fusion.5.place, bf16[1,64,64,128]{3,2,1,0:T(8,128)(2,1)S(1)} %copy-done.5, bf16[64,64,128]{2,1,0:T(8,128)(2,1)} %collective-permute-done.11.rest_0_, bf16[64,512,128]{2,1,0:T(8,128)(2,1)} %shard_map.58.rest_1_), custom_call_target="tpu_custom_call", output_to_operand_aliasing={{}: (3, {})} | custom-call | tf_op jit(solution)/shard_map/pallas_call | solution.py:230
  216.3 3.5 %shard_map.60.rest_1_ = bf16[64,512,128]{2,1,0:T(8,128)(2,1)} custom-call(s32[2]{0:T(128)S(1)} %pad_add_fusion.4.place, bf16[1,64,64,128]{3,2,1,0:T(8,128)(2,1)S(1)} %copy-done.4, bf16[64,64,128]{2,1,0:T(8,128)(2,1)} %collective-permute-done.9.rest_0_, bf16[64,512,128]{2,1,0:T(8,128)(2,1)} %shard_map.59.rest_1_), custom_call_target="tpu_custom_call", output_to_operand_aliasing={{}: (3, {})} | custom-call | tf_op jit(solution)/shard_map/pallas_call | solution.py:230
  219.9 51.3 %collective-permute-done.8.rest_0_ = bf16[64,64,128]{2,1,0:T(8,128)(2,1)} collective-permute-done((bf16[64,64,128]{2,1,0:T(8,128)(2,1)}, bf16[64,64,128]{2,1,0:T(8,128)(2,1)}, u32[]{:S(2)}, u32[]{:S(2)}) %collective-permute-start.8) | collective-permute-done | bytes 1048608 | tf_op jit(solution)/shard_map/ppermute | solution.py:266
  271.1 3.5 %shard_map.61.rest_1_ = bf16[64,512,128]{2,1,0:T(8,128)(2,1)} custom-call(s32[2]{0:T(128)S(1)} %pad_add_fusion.3.place, bf16[1,64,64,128]{3,2,1,0:T(8,128)(2,1)S(1)} %copy-done.3, bf16[64,64,128]{2,1,0:T(8,128)(2,1)} %collective-permute-done.8.rest_0_, bf16[64,512,128]{2,1,0:T(8,128)(2,1)} %shard_map.60.rest_1_), custom_call_target="tpu_custom_call", output_to_operand_aliasing={{}: (3, {})} | custom-call | tf_op jit(solution)/shard_map/pallas_call | solution.py:230
  274.6 3.5 %shard_map.62.rest_1_ = bf16[64,512,128]{2,1,0:T(8,128)(2,1)} custom-call(s32[2]{0:T(128)S(1)} %pad_add_fusion.2.place, bf16[1,64,64,128]{3,2,1,0:T(8,128)(2,1)S(1)} %copy-done.1, bf16[64,64,128]{2,1,0:T(8,128)(2,1)} %collective-permute-done.6.rest_0_, bf16[64,512,128]{2,1,0:T(8,128)(2,1)} %shard_map.61.rest_1_), custom_call_target="tpu_custom_call", output_to_operand_aliasing={{}: (3, {})} | custom-call | tf_op jit(solution)/shard_map/pallas_call | solution.py:230
  278.1 15.1 %collective-permute-done.5.rest_0_ = bf16[64,64,128]{2,1,0:T(8,128)(2,1)} collective-permute-done((bf16[64,64,128]{2,1,0:T(8,128)(2,1)}, bf16[64,64,128]{2,1,0:T(8,128)(2,1)}, u32[]{:S(2)}, u32[]{:S(2)}) %collective-permute-start.5) | collective-permute-done | bytes 1048608 | tf_op jit(solution)/shard_map/ppermute | solution.py:266
  293.2 3.6 %shard_map.63.rest_1_ = bf16[64,512,128]{2,1,0:T(8,128)(2,1)} custom-call(s32[2]{0:T(128)S(1)} %pad_add_fusion.1.place, bf16[1,64,64,128]{3,2,1,0:T(8,128)(2,1)S(1)} %get-tuple-element.31.own, bf16[64,64,128]{2,1,0:T(8,128)(2,1)} %collective-permute-done.5.rest_0_, bf16[64,512,128]{2,1,0:T(8,128)(2,1)} %shard_map.62.rest_1_), custom_call_target="tpu_custom_call", output_to_operand_aliasing={{}: (3, {})} | custom-call | tf_op jit(solution)/shard_map/pallas_call | solution.py:230
  296.8 3.6 %shard_map.64.one.two.odd.even.rest_0_.three = bf16[64,512,128]{2,1,0:T(8,128)(2,1)} custom-call(s32[2]{0:T(128)S(1)} %pad_add_fusion.place, bf16[1,64,64,128]{3,2,1,0:T(8,128)(2,1)S(1)} %get-tuple-element.29.own, bf16[64,64,128]{2,1,0:T(8,128)(2,1)} %collective-permute-done.3.rest_0_, ...), custom_call_target="tpu_custom_call", output_to_operand_aliasing={{}: (3, {})} | custom-call | tf_op jit(solution)/shard_map/pallas_call | solution.py:230
  301.5 1.3 fusion
  302.7 3.0 collective-permute-done.15
  305.8 1.9 collective-permute-start.16
  307.8 4.8 %collective-permute-start.17 = (bf16[4,520,128]{2,1,0:T(8,128)(2,1)S(1)}, bf16[4,520,128]{2,1,0:T(8,128)(2,1)S(1)}, u32[]{:S(2)}, u32[]{:S(2)}) collective-permute-start(bf16[4,520,128]{2,1,0:T(8,128)(2,1)S(1)} %pad_maximum_fusion.5), channel_id=1, source_target_pairs={{2,0},{4,2},{6,4},{8,6},{10,8},{12,10},{14,12},{16,14},{18,16},{20... | collective-permute-start | bytes 1597448 | tf_op jit(solution)/shard_map/ppermute | solution.py:176
  312.6 18.1 %shard_map.65.rest_1_ = bf16[64,512,128]{2,1,0:T(8,128)(2,1)} custom-call(s32[1]{0:T(128)} %bitcast.me, bf16[64,512,128]{2,1,0:T(8,128)(2,1)} %shard_map.64.one.two.odd.even.rest_0_.three, bf16[64,512,128]{2,1,0:T(8,128)(2,1)} %shard_map.64.one.two.odd.even.rest_0_.three, bf16[64,512,128]{2,1,0:T(8,128)(2,1)} %shard_map.64.one.two.odd.even.rest_0_.three, ...), custom_call_target="tpu_custom_call" | custom-call | flops 9663676416 | bytes 25165824 | tf_op jit(solution)/shard_map/pallas_call | solution.py:109
  330.9 9.0 %shard_map.66 = bf16[64,512,128]{2,1,0:T(8,128)(2,1)} custom-call(s32[1]{0:T(128)} %bitcast.me, bf16[4,520,128]{2,1,0:T(8,128)(2,1)S(1)} %collective-permute-done.16.low, bf16[4,520,128]{2,1,0:T(8,128)(2,1)S(1)} %collective-permute-done.17.high, bf16[64,512,128]{2,1,0:T(8,128)(2,1)} %shard_map.64.one.two.odd.even.rest_0_.three, ...), custom_call_target="tpu_custom_call", output_to_operand_aliasing={{}: (11, {})} | custom-call | flops 3221225472 | bytes 8388608 | tf_op jit(solution)/shard_map/pallas_call | solution.py:138
  (83 shorter events, 10.8 us)
Async XLA Ops:
  0.0 3.9 %copy-start.10 = (bf16[3,3,128,128]{3,2,1,0:T(8,128)(2,1)S(1)}, bf16[3,3,128,128]{3,2,1,0:T(8,128)(2,1)}, u32[]{:S(2)}) copy-start(bf16[3,3,128,128]{3,2,1,0:T(8,128)(2,1)} %param.8) | copy-start | bytes 884740
  0.0 3.9 %copy-start.11 = (bf16[3,3,128,128]{3,2,1,0:T(8,128)(2,1)S(1)}, bf16[3,3,128,128]{3,2,1,0:T(8,128)(2,1)}, u32[]{:S(2)}) copy-start(bf16[3,3,128,128]{3,2,1,0:T(8,128)(2,1)} %param.6) | copy-start | bytes 884740
  1.1 4.8 %collective-permute-start = (bf16[64,4,128]{2,1,0:T(4,128)(2,1)S(1)}, bf16[64,4,128]{2,1,0:T(4,128)(2,1)S(1)}, u32[]{:S(2)}, u32[]{:S(2)}) collective-permute-start(bf16[64,4,128]{2,1,0:T(4,128)(2,1)S(1)} %slice_select_fusion.1), channel_id=1, source_target_pairs={{0,1},{1,0},{2,3},{3,2},{4,5},{5,4},{6,7},{7,6},{8,9},{9,8},{10,11... | collective-permute-start | bytes 196616 | tf_op jit(solution)/shard_map/ppermute | solution.py:184
  5.9 4.7 %copy-start.9 = (f32[128]{0:T(128)S(1)}, f32[128]{0:T(128)}, u32[]{:S(2)}) copy-start(f32[128]{0:T(128)} %param.7) | copy-start | bytes 1540
  5.9 4.7 %copy-start.7 = (bf16[1536,256]{1,0:T(8,128)(2,1)S(1)}, bf16[1536,256]{1,0:T(8,128)(2,1)}, u32[]{:S(2)}) copy-start(bf16[1536,256]{1,0:T(8,128)(2,1)} %pad_maximum_fusion.weights) | copy-start | bytes 2359300
  6.0 25.1 %collective-permute-start.2 = (bf16[4,520,128]{2,1,0:T(8,128)(2,1)S(1)}, bf16[4,520,128]{2,1,0:T(8,128)(2,1)S(1)}, u32[]{:S(2)}, u32[]{:S(2)}) collective-permute-start(bf16[4,520,128]{2,1,0:T(8,128)(2,1)S(1)} %pad_maximum_fusion.3), channel_id=1, source_target_pairs={{2,0},{4,2},{6,4},{8,6},{10,8},{12,10},{14,12},{16,14},{18,16},{20... | collective-permute-start | bytes 1597448 | tf_op jit(solution)/shard_map/ppermute | solution.py:176
  8.7 22.5 %collective-permute-start.1 = (bf16[4,520,128]{2,1,0:T(8,128)(2,1)S(1)}, bf16[4,520,128]{2,1,0:T(8,128)(2,1)S(1)}, u32[]{:S(2)}, u32[]{:S(2)}) collective-permute-start(bf16[4,520,128]{2,1,0:T(8,128)(2,1)S(1)} %pad_maximum_fusion.2), channel_id=1, source_target_pairs={{0,2},{2,4},{4,6},{6,8},{8,10},{10,12},{12,14},{14,16},{16,18},{18... | collective-permute-start | bytes 1597448 | tf_op jit(solution)/shard_map/ppermute | solution.py:176
  30.1 1.0 copy-start.2
  40.0 1.0 copy-start
  41.0 48.5 %collective-permute-start.13 = (bf16[64,64,128]{2,1,0:T(8,128)(2,1)S(1)}, bf16[64,64,128]{2,1,0:T(8,128)(2,1)}, u32[]{:S(2)}, u32[]{:S(2)}) collective-permute-start(bf16[64,64,128]{2,1,0:T(8,128)(2,1)S(1)} %bitcast.42), channel_id=1, source_target_pairs={{0,1},{1,0},{2,3},{3,2},{4,5},{5,4},{6,7},{7,6},{8,9},{9,8},{10,11... | collective-permute-start | bytes 3145736 | tf_op jit(solution)/shard_map/ppermute | solution.py:266
  41.8 70.2 %collective-permute-start.10 = (bf16[64,64,128]{2,1,0:T(8,128)(2,1)S(1)}, bf16[64,64,128]{2,1,0:T(8,128)(2,1)}, u32[]{:S(2)}, u32[]{:S(2)}) collective-permute-start(bf16[64,64,128]{2,1,0:T(8,128)(2,1)S(1)} %bitcast.44), channel_id=1, source_target_pairs={{0,1},{1,0},{2,3},{3,2},{4,5},{5,4},{6,7},{7,6},{8,9},{9,8},{10,11... | collective-permute-start | bytes 3145736 | tf_op jit(solution)/shard_map/ppermute | solution.py:266
  43.0 69.0 %collective-permute-start.12 = (bf16[64,64,128]{2,1,0:T(8,128)(2,1)S(1)}, bf16[64,64,128]{2,1,0:T(8,128)(2,1)}, u32[]{:S(2)}, u32[]{:S(2)}) collective-permute-start(bf16[64,64,128]{2,1,0:T(8,128)(2,1)S(1)} %bitcast.43), channel_id=1, source_target_pairs={{0,2},{1,18},{2,4},{3,20},{4,6},{5,22},{6,8},{7,24},{8,10},{9,26},... | collective-permute-start | bytes 3145736 | tf_op jit(solution)/shard_map/ppermute | solution.py:266
  43.8 109.0 %collective-permute-start.7 = (bf16[64,64,128]{2,1,0:T(8,128)(2,1)}, bf16[64,64,128]{2,1,0:T(8,128)(2,1)}, u32[]{:S(2)}, u32[]{:S(2)}) collective-permute-start(bf16[64,64,128]{2,1,0:T(8,128)(2,1)} %bitcast.46), channel_id=1, source_target_pairs={{0,1},{1,0},{2,3},{3,2},{4,5},{5,4},{6,7},{7,6},{8,9},{9,8},{10,11... | collective-permute-start | bytes 3145736 | tf_op jit(solution)/shard_map/ppermute | solution.py:266
  44.4 130.8 %collective-permute-start.4 = (bf16[64,64,128]{2,1,0:T(8,128)(2,1)}, bf16[64,64,128]{2,1,0:T(8,128)(2,1)}, u32[]{:S(2)}, u32[]{:S(2)}) collective-permute-start(bf16[64,64,128]{2,1,0:T(8,128)(2,1)} %bitcast.48), channel_id=1, source_target_pairs={{0,1},{1,0},{2,3},{3,2},{4,5},{5,4},{6,7},{7,6},{8,9},{9,8},{10,11... | collective-permute-start | bytes 3145736 | tf_op jit(solution)/shard_map/ppermute | solution.py:266
  89.5 109.3 %collective-permute-start.14 = (bf16[64,64,128]{2,1,0:T(8,128)(2,1)}, bf16[64,64,128]{2,1,0:T(8,128)(2,1)}, u32[]{:S(2)}, u32[]{:S(2)}) collective-permute-start(bf16[64,64,128]{2,1,0:T(8,128)(2,1)} %collective-permute-done.13), channel_id=1, source_target_pairs={{1,0},{0,16},{3,2},{2,18},{5,4},{4,20},{7,6},{6,22},{9,8},{8,24},{... | collective-permute-start | bytes 3145736 | tf_op jit(solution)/shard_map/ppermute | solution.py:266
  111.9 90.5 %collective-permute-start.11 = (bf16[64,64,128]{2,1,0:T(8,128)(2,1)}, bf16[64,64,128]{2,1,0:T(8,128)(2,1)}, u32[]{:S(2)}, u32[]{:S(2)}) collective-permute-start(bf16[64,64,128]{2,1,0:T(8,128)(2,1)} %collective-permute-done.10), channel_id=1, source_target_pairs={{1,4},{0,20},{3,6},{2,22},{5,8},{4,24},{7,10},{6,26},{9,12},{8,28}... | collective-permute-start | bytes 3145736 | tf_op jit(solution)/shard_map/ppermute | solution.py:266
  112.0 104.4 %collective-permute-start.9 = (bf16[64,64,128]{2,1,0:T(8,128)(2,1)}, bf16[64,64,128]{2,1,0:T(8,128)(2,1)}, u32[]{:S(2)}, u32[]{:S(2)}) collective-permute-start(bf16[64,64,128]{2,1,0:T(8,128)(2,1)} %bitcast.45), channel_id=1, source_target_pairs={{0,6},{1,22},{2,8},{3,24},{4,10},{5,26},{6,12},{7,28},{8,14},{9,30... | collective-permute-start | bytes 3145736 | tf_op jit(solution)/shard_map/ppermute | solution.py:266
  152.7 121.9 %collective-permute-start.6 = (bf16[64,64,128]{2,1,0:T(8,128)(2,1)}, bf16[64,64,128]{2,1,0:T(8,128)(2,1)}, u32[]{:S(2)}, u32[]{:S(2)}) collective-permute-start(bf16[64,64,128]{2,1,0:T(8,128)(2,1)} %bitcast.47), channel_id=1, source_target_pairs={{0,10},{1,26},{2,12},{3,28},{4,14},{5,30},{6,0},{7,16},{8,2},{9,18... | collective-permute-start | bytes 3145736 | tf_op jit(solution)/shard_map/ppermute | solution.py:266
  175.2 121.6 %collective-permute-start.3 = (bf16[64,64,128]{2,1,0:T(8,128)(2,1)}, bf16[64,64,128]{2,1,0:T(8,128)(2,1)}, u32[]{:S(2)}, u32[]{:S(2)}) collective-permute-start(bf16[64,64,128]{2,1,0:T(8,128)(2,1)} %bitcast.49), channel_id=1, source_target_pairs={{0,14},{1,30},{2,0},{3,16},{4,2},{5,18},{6,4},{7,20},{8,6},{9,22},... | collective-permute-start | bytes 3145736 | tf_op jit(solution)/shard_map/ppermute | solution.py:266
  198.8 72.3 %collective-permute-start.8 = (bf16[64,64,128]{2,1,0:T(8,128)(2,1)}, bf16[64,64,128]{2,1,0:T(8,128)(2,1)}, u32[]{:S(2)}, u32[]{:S(2)}) collective-permute-start(bf16[64,64,128]{2,1,0:T(8,128)(2,1)} %collective-permute-done.7), channel_id=1, source_target_pairs={{1,8},{0,24},{3,10},{2,26},{5,12},{4,28},{7,14},{6,30},{9,0},{8,16... | collective-permute-start | bytes 3145736 | tf_op jit(solution)/shard_map/ppermute | solution.py:266
  202.4 90.8 %collective-permute-start.5 = (bf16[64,64,128]{2,1,0:T(8,128)(2,1)}, bf16[64,64,128]{2,1,0:T(8,128)(2,1)}, u32[]{:S(2)}, u32[]{:S(2)}) collective-permute-start(bf16[64,64,128]{2,1,0:T(8,128)(2,1)} %collective-permute-done.4), channel_id=1, source_target_pairs={{1,12},{0,28},{3,14},{2,30},{5,0},{4,16},{7,2},{6,18},{9,4},{8,20}... | collective-permute-start | bytes 3145736 | tf_op jit(solution)/shard_map/ppermute | solution.py:266
  205.6 3.6 %copy-start.6 = (bf16[1,64,64,128]{3,2,1,0:T(8,128)(2,1)S(1)}, bf16[1,64,64,128]{3,2,1,0:T(8,128)(2,1)}, u32[]{:S(2)}) copy-start(bf16[1,64,64,128]{3,2,1,0:T(8,128)(2,1)} %get-tuple-element.30.own) | copy-start | bytes 3145732
  209.2 3.6 %copy-start.5 = (bf16[1,64,64,128]{3,2,1,0:T(8,128)(2,1)S(1)}, bf16[1,64,64,128]{3,2,1,0:T(8,128)(2,1)}, u32[]{:S(2)}) copy-start(bf16[1,64,64,128]{3,2,1,0:T(8,128)(2,1)} %get-tuple-element.32.own) | copy-start | bytes 3145732
  212.8 3.5 %copy-start.4 = (bf16[1,64,64,128]{3,2,1,0:T(8,128)(2,1)S(1)}, bf16[1,64,64,128]{3,2,1,0:T(8,128)(2,1)}, u32[]{:S(2)}) copy-start(bf16[1,64,64,128]{3,2,1,0:T(8,128)(2,1)} %get-tuple-element.34.own) | copy-start | bytes 3145732
  216.3 54.8 %copy-start.3 = (bf16[1,64,64,128]{3,2,1,0:T(8,128)(2,1)S(1)}, bf16[1,64,64,128]{3,2,1,0:T(8,128)(2,1)}, u32[]{:S(2)}) copy-start(bf16[1,64,64,128]{3,2,1,0:T(8,128)(2,1)} %get-tuple-element.35.own) | copy-start | bytes 3145732
  219.9 54.8 %copy-start.1 = (bf16[1,64,64,128]{3,2,1,0:T(8,128)(2,1)S(1)}, bf16[1,64,64,128]{3,2,1,0:T(8,128)(2,1)}, u32[]{:S(2)}) copy-start(bf16[1,64,64,128]{3,2,1,0:T(8,128)(2,1)} %copy-done) | copy-start | bytes 3145732
  301.4 4.3 %collective-permute-start.15 = (bf16[64,4,128]{2,1,0:T(4,128)(2,1)S(1)}, bf16[64,4,128]{2,1,0:T(4,128)(2,1)S(1)}, u32[]{:S(2)}, u32[]{:S(2)}) collective-permute-start(bf16[64,4,128]{2,1,0:T(4,128)(2,1)S(1)} %slice_select_fusion), channel_id=1, source_target_pairs={{0,1},{1,0},{2,3},{3,2},{4,5},{5,4},{6,7},{7,6},{8,9},{9,8},{10,11... | collective-permute-start | bytes 196616 | tf_op jit(solution)/shard_map/ppermute | solution.py:184
  302.7 9.9 %copy-start.8 = (f32[128]{0:T(128)S(1)}, f32[128]{0:T(128)}, u32[]{:S(2)}) copy-start(f32[128]{0:T(128)} %param.9) | copy-start | bytes 1540
  305.8 24.9 %collective-permute-start.16 = (bf16[4,520,128]{2,1,0:T(8,128)(2,1)S(1)}, bf16[4,520,128]{2,1,0:T(8,128)(2,1)S(1)}, u32[]{:S(2)}, u32[]{:S(2)}) collective-permute-start(bf16[4,520,128]{2,1,0:T(8,128)(2,1)S(1)} %pad_maximum_fusion.4), channel_id=1, source_target_pairs={{0,2},{2,4},{4,6},{6,8},{8,10},{10,12},{12,14},{14,16},{16,18},{18... | collective-permute-start | bytes 1597448 | tf_op jit(solution)/shard_map/ppermute | solution.py:176
  307.8 22.9 %collective-permute-start.17 = (bf16[4,520,128]{2,1,0:T(8,128)(2,1)S(1)}, bf16[4,520,128]{2,1,0:T(8,128)(2,1)S(1)}, u32[]{:S(2)}, u32[]{:S(2)}) collective-permute-start(bf16[4,520,128]{2,1,0:T(8,128)(2,1)S(1)} %pad_maximum_fusion.5), channel_id=1, source_target_pairs={{2,0},{4,2},{6,4},{8,6},{10,8},{12,10},{14,12},{16,14},{18,16},{20... | collective-permute-start | bytes 1597448 | tf_op jit(solution)/shard_map/ppermute | solution.py:176

commit v3 on v2

--- a/solution.py
+++ b/solution.py
@@ -286,7 +286,7 @@
                 pairs = [(device(a, m, 1 - j), device(j, m + s, a)) for a, m, j in places]
                 landed[s] = [(send(hop, pairs),)]
     result = None
-    for s in [s for s in range(count) if s in landed] + [s for s in landed if s > 7]:
+    for s in sorted(landed, key=lambda s: s ^ 1):
         i, n = where[-s % count]
         place = jnp.stack([lax.rem(me[0] - s + count, count), mine])
         result = symmetrize(result, shape, pieces[i], n, landed[s], place)

time: 340 us -> 364 us (1.071); the launches traced: 340 us -> 359 us
  waiting for transfers between devices: 197 us -> 218 us
    ppermute x12, waiting for transfers between devices: 194 us -> 217 us  [send(): return lax.ppermute(block, ('row', 'col'), pairs)]
    ppermute x12, starting transfers between devices: 35.4 us -> 28.7 us  [send(): return lax.ppermute(block, ('row', 'col'), pairs)]
    ppermute x2, starting transfers between devices: 1.63 us -> 6.45 us  [halos(): edge = lax.ppermute(edge, 'col', [(0, 1), (1, 0)])]
  transfers between devices with their start and end apart: 18 -> 18, of which waited for: 7 -> 8; matrix products, arithmetic and copies ran while one was open for 2% -> 2% of each run, Pallas kernels for 18% -> 17%
where the time goes in v3:
time: 364 us; the launch traced here: 359 us
  waiting for transfers between devices  218 us (60%)
  Pallas kernels  83 us (23%)
  starting transfers between devices  46.2 us (13%)
  local copies, waits for them, and re-layouts  6.86 us (2%)
  other arithmetic  4.4 us (1%)
    ppermute x12, waiting for transfers between devices, send(): return lax.ppermute(block, ('row', 'col'), pairs)  217 us
    pallas_call x2, Pallas kernels, conv(): pl.pallas_call(functools.partial(inner_kernel, finish), grid_spec=pltpu.P...  37.7 us
    ppermute x12, starting transfers between devices, send(): return lax.ppermute(block, ('row', 'col'), pairs)  28.7 us
    pallas_call x8, Pallas kernels, symmetrize(): pl.pallas_call(functools.partial(mirror_kernel, sizes), grid_spec=pltpu.P...  27.6 us
    pallas_call x2, Pallas kernels, conv(): pl.pallas_call(functools.partial(outer_kernel, finish), grid_spec=pltpu.P...  17.7 us
    ppermute x4, starting transfers between devices, move(): lax.ppermute(part, axis, [(i, i + 1) if up else (i + 1, i) for i in range...  11 us
  transfers between devices with their start and end apart: 18, of which 8 were waited for; matrix products, arithmetic and copies ran while one was open for 2% of the time, Pallas kernels for 17%

profile of v3, /device:TPU:16, one launch (start us, length us, event | category | flops | bytes accessed | tf_op | source)
XLA Modules:
  0.0 359.2 jit_solution(9548472518189253574)
XLA Ops:
  1.1 1.6 collective-permute-start
  2.7 1.3 fusion.1
  5.5 2.1 collective-permute-start.2
  7.7 2.2 collective-permute-start.1
  9.9 19.6 %shard_map.55 = (bf16[1,64,64,128]{3,2,1,0:T(8,128)(2,1)S(1)}, bf16[1,64,64,128]{3,2,1,0:T(8,128)(2,1)S(1)}, bf16[1,64,64,128]{3,2,1,0:T(8,128)(2,1)}, bf16[1,64...) custom-call(s32[1]{0:T(128)} %bitcast.me, ...), custom_call_target="tpu_custom_call" | custom-call | flops 9663676416 | bytes 25165824 | tf_op jit(solution)/shard_map/pallas_call | solution.py:109
  30.8 8.8 %shard_map.56 = (bf16[1,64,64,128]{3,2,1,0:T(8,128)(2,1)S(1)}, bf16[1,64,64,128]{3,2,1,0:T(8,128)(2,1)S(1)}, bf16[1,64,64,128]{3,2,1,0:T(8,128)(2,1)}, bf16[1,64...) custom-call(s32[1]{0:T(128)} %bitcast.me, ...), custom_call_target="tpu_custom_call", output_to_operand_aliasing={{0}: (10, {}), {1}: (11, {}), {2}: (12, {}), {3}: (13, {}),... | custom-call | flops 3221225472 | bytes 8388608 | tf_op jit(solution)/shard_map/pallas_call | solution.py:138
  39.6 2.1 collective-permute-start.14
  42.3 2.8 collective-permute-start.11
  45.1 2.0 collective-permute-start.6
  47.1 64.0 %collective-permute-done.14.rest_0_ = bf16[64,64,128]{2,1,0:T(8,128)(2,1)S(1)} collective-permute-done((bf16[64,64,128]{2,1,0:T(8,128)(2,1)S(1)}, bf16[64,64,128]{2,1,0:T(8,128)(2,1)S(1)}, u32[]{:S(2)}, u32[]{:S(2)}) %collective-permute-start.14) | collective-permute-done | bytes 1048608 | tf_op jit(solution)/shard_map/ppermute | solution.py:266
  112.2 2.0 collective-permute-start.13
  114.2 43.6 %collective-permute-done.11.rest_0_ = bf16[64,64,128]{2,1,0:T(8,128)(2,1)} collective-permute-done((bf16[64,64,128]{2,1,0:T(8,128)(2,1)}, bf16[64,64,128]{2,1,0:T(8,128)(2,1)}, u32[]{:S(2)}, u32[]{:S(2)}) %collective-permute-start.11) | collective-permute-done | bytes 1048608 | tf_op jit(solution)/shard_map/ppermute | solution.py:266
  157.8 15.7 %collective-permute-start.10 = (bf16[64,64,128]{2,1,0:T(8,128)(2,1)}, bf16[64,64,128]{2,1,0:T(8,128)(2,1)}, u32[]{:S(2)}, u32[]{:S(2)}) collective-permute-start(bf16[64,64,128]{2,1,0:T(8,128)(2,1)} %collective-permute-done.9), channel_id=1, source_target_pairs={{1,4},{0,20},{3,6},{2,22},{5,8},{4,24},{7,10},{6,26},{9,12},{8,28}... | collective-permute-start | bytes 3145736 | tf_op jit(solution)/shard_map/ppermute | solution.py:266
  173.5 47.0 %collective-permute-done.3 = bf16[64,64,128]{2,1,0:T(8,128)(2,1)} collective-permute-done((bf16[64,64,128]{2,1,0:T(8,128)(2,1)}, bf16[64,64,128]{2,1,0:T(8,128)(2,1)}, u32[]{:S(2)}, u32[]{:S(2)}) %collective-permute-start.3) | collective-permute-done | bytes 1048608 | tf_op jit(solution)/shard_map/ppermute | solution.py:266
  220.5 3.4 collective-permute-start.7
  226.9 2.3 shard_map.57.rest_1_
  229.2 3.5 shard_map.58.rest_1_
  232.7 3.5 shard_map.59.rest_1_
  236.2 38.8 %collective-permute-done.10.rest_0_ = bf16[64,64,128]{2,1,0:T(8,128)(2,1)} collective-permute-done((bf16[64,64,128]{2,1,0:T(8,128)(2,1)}, bf16[64,64,128]{2,1,0:T(8,128)(2,1)}, u32[]{:S(2)}, u32[]{:S(2)}) %collective-permute-start.10) | collective-permute-done | bytes 1048608 | tf_op jit(solution)/shard_map/ppermute | solution.py:266
  275.0 3.5 shard_map.60.rest_1_
  278.5 3.9 %shard_map.61.rest_1_ = bf16[64,512,128]{2,1,0:T(8,128)(2,1)} custom-call(s32[2]{0:T(128)S(1)} %pad_add_fusion.3.place, bf16[1,64,64,128]{3,2,1,0:T(8,128)(2,1)} %get-tuple-element.34.own, bf16[64,64,128]{2,1,0:T(8,128)(2,1)} %collective-permute-done.8.rest_0_, bf16[64,512,128]{2,1,0:T(8,128)(2,1)} %shard_map.60.rest_1_), custom_call_target="tpu_custom_call", output_to_operand_aliasing={{}: (3, {})} | custom-call | tf_op jit(solution)/shard_map/pallas_call | solution.py:230
  282.4 13.1 %collective-permute-done.7.rest_0_ = bf16[64,64,128]{2,1,0:T(8,128)(2,1)} collective-permute-done((bf16[64,64,128]{2,1,0:T(8,128)(2,1)}, bf16[64,64,128]{2,1,0:T(8,128)(2,1)}, u32[]{:S(2)}, u32[]{:S(2)}) %collective-permute-start.7) | collective-permute-done | bytes 1048608 | tf_op jit(solution)/shard_map/ppermute | solution.py:266
  295.5 3.5 shard_map.62.rest_1_
  299.0 3.5 shard_map.63.rest_1_
  302.5 10.4 %collective-permute-done.4.rest_0_ = bf16[64,64,128]{2,1,0:T(8,128)(2,1)} collective-permute-done((bf16[64,64,128]{2,1,0:T(8,128)(2,1)}, bf16[64,64,128]{2,1,0:T(8,128)(2,1)}, u32[]{:S(2)}, u32[]{:S(2)}) %collective-permute-start.4) | collective-permute-done | bytes 1048608 | tf_op jit(solution)/shard_map/ppermute | solution.py:266
  313.0 3.9 %shard_map.64.one.two.odd.even.rest_0_.three = bf16[64,512,128]{2,1,0:T(8,128)(2,1)} custom-call(s32[2]{0:T(128)S(1)} %pad_add_fusion.place, bf16[1,64,64,128]{3,2,1,0:T(8,128)(2,1)} %get-tuple-element.29.own, bf16[64,64,128]{2,1,0:T(8,128)(2,1)} %collective-permute-done.4.rest_0_, ...), custom_call_target="tpu_custom_call", output_to_operand_aliasing={{}: (3, {})} | custom-call | tf_op jit(solution)/shard_map/pallas_call | solution.py:230
  317.9 4.9 %collective-permute-start.15 = (bf16[64,4,128]{2,1,0:T(4,128)(2,1)S(1)}, bf16[64,4,128]{2,1,0:T(4,128)(2,1)S(1)}, u32[]{:S(2)}, u32[]{:S(2)}) collective-permute-start(bf16[64,4,128]{2,1,0:T(4,128)(2,1)S(1)} %slice_select_fusion), channel_id=1, source_target_pairs={{0,1},{1,0},{2,3},{3,2},{4,5},{5,4},{6,7},{7,6},{8,9},{9,8},{10,11... | collective-permute-start | bytes 196616 | tf_op jit(solution)/shard_map/ppermute | solution.py:184
  322.8 1.3 fusion
  325.2 1.9 collective-permute-start.16
  327.2 4.8 %collective-permute-start.17 = (bf16[4,520,128]{2,1,0:T(8,128)(2,1)S(1)}, bf16[4,520,128]{2,1,0:T(8,128)(2,1)S(1)}, u32[]{:S(2)}, u32[]{:S(2)}) collective-permute-start(bf16[4,520,128]{2,1,0:T(8,128)(2,1)S(1)} %pad_maximum_fusion.5), channel_id=1, source_target_pairs={{2,0},{4,2},{6,4},{8,6},{10,8},{12,10},{14,12},{16,14},{18,16},{20... | collective-permute-start | bytes 1597448 | tf_op jit(solution)/shard_map/ppermute | solution.py:176
  331.9 18.1 %shard_map.65.rest_1_ = bf16[64,512,128]{2,1,0:T(8,128)(2,1)} custom-call(s32[1]{0:T(128)} %bitcast.me, bf16[64,512,128]{2,1,0:T(8,128)(2,1)} %shard_map.64.one.two.odd.even.rest_0_.three, bf16[64,512,128]{2,1,0:T(8,128)(2,1)} %shard_map.64.one.two.odd.even.rest_0_.three, bf16[64,512,128]{2,1,0:T(8,128)(2,1)} %shard_map.64.one.two.odd.even.rest_0_.three, ...), custom_call_target="tpu_custom_call" | custom-call | flops 9663676416 | bytes 25165824 | tf_op jit(solution)/shard_map/pallas_call | solution.py:109
  350.2 8.9 %shard_map.66 = bf16[64,512,128]{2,1,0:T(8,128)(2,1)} custom-call(s32[1]{0:T(128)} %bitcast.me, bf16[4,520,128]{2,1,0:T(8,128)(2,1)S(1)} %collective-permute-done.16.low, bf16[4,520,128]{2,1,0:T(8,128)(2,1)S(1)} %collective-permute-done.17.high, bf16[64,512,128]{2,1,0:T(8,128)(2,1)} %shard_map.64.one.two.odd.even.rest_0_.three, ...), custom_call_target="tpu_custom_call", output_to_operand_aliasing={{}: (11, {})} | custom-call | flops 3221225472 | bytes 8388608 | tf_op jit(solution)/shard_map/pallas_call | solution.py:138
  (81 shorter events, 10.7 us)
Async XLA Ops:
  0.0 3.9 %copy-start.9 = (bf16[3,3,128,128]{3,2,1,0:T(8,128)(2,1)S(1)}, bf16[3,3,128,128]{3,2,1,0:T(8,128)(2,1)}, u32[]{:S(2)}) copy-start(bf16[3,3,128,128]{3,2,1,0:T(8,128)(2,1)} %param.8) | copy-start | bytes 884740
  0.0 3.9 %copy-start.10 = (bf16[3,3,128,128]{3,2,1,0:T(8,128)(2,1)S(1)}, bf16[3,3,128,128]{3,2,1,0:T(8,128)(2,1)}, u32[]{:S(2)}) copy-start(bf16[3,3,128,128]{3,2,1,0:T(8,128)(2,1)} %param.6) | copy-start | bytes 884740
  1.1 4.3 %collective-permute-start = (bf16[64,4,128]{2,1,0:T(4,128)(2,1)S(1)}, bf16[64,4,128]{2,1,0:T(4,128)(2,1)S(1)}, u32[]{:S(2)}, u32[]{:S(2)}) collective-permute-start(bf16[64,4,128]{2,1,0:T(4,128)(2,1)S(1)} %slice_select_fusion.1), channel_id=1, source_target_pairs={{0,1},{1,0},{2,3},{3,2},{4,5},{5,4},{6,7},{7,6},{8,9},{9,8},{10,11... | collective-permute-start | bytes 196616 | tf_op jit(solution)/shard_map/ppermute | solution.py:184
  5.0 4.9 %copy-start.8 = (f32[128]{0:T(128)S(1)}, f32[128]{0:T(128)}, u32[]{:S(2)}) copy-start(f32[128]{0:T(128)} %param.7) | copy-start | bytes 1540
  5.5 25.0 %collective-permute-start.2 = (bf16[4,520,128]{2,1,0:T(8,128)(2,1)S(1)}, bf16[4,520,128]{2,1,0:T(8,128)(2,1)S(1)}, u32[]{:S(2)}, u32[]{:S(2)}) collective-permute-start(bf16[4,520,128]{2,1,0:T(8,128)(2,1)S(1)} %pad_maximum_fusion.3), channel_id=1, source_target_pairs={{2,0},{4,2},{6,4},{8,6},{10,8},{12,10},{14,12},{16,14},{18,16},{20... | collective-permute-start | bytes 1597448 | tf_op jit(solution)/shard_map/ppermute | solution.py:176
  7.7 22.9 %collective-permute-start.1 = (bf16[4,520,128]{2,1,0:T(8,128)(2,1)S(1)}, bf16[4,520,128]{2,1,0:T(8,128)(2,1)S(1)}, u32[]{:S(2)}, u32[]{:S(2)}) collective-permute-start(bf16[4,520,128]{2,1,0:T(8,128)(2,1)S(1)} %pad_maximum_fusion.2), channel_id=1, source_target_pairs={{0,2},{2,4},{4,6},{6,8},{8,10},{10,12},{12,14},{14,16},{16,18},{18... | collective-permute-start | bytes 1597448 | tf_op jit(solution)/shard_map/ppermute | solution.py:176
  29.6 1.0 copy-start.1
  39.6 186.1 %copy-start = (bf16[1,64,64,128]{3,2,1,0:T(8,128)(2,1)S(1)}, bf16[1,64,64,128]{3,2,1,0:T(8,128)(2,1)}, u32[]{:S(2)}) copy-start(bf16[1,64,64,128]{3,2,1,0:T(8,128)(2,1)} %get-tuple-element.32.own) | copy-start | bytes 3145732
  39.6 71.6 %collective-permute-start.14 = (bf16[64,64,128]{2,1,0:T(8,128)(2,1)S(1)}, bf16[64,64,128]{2,1,0:T(8,128)(2,1)S(1)}, u32[]{:S(2)}, u32[]{:S(2)}) collective-permute-start(bf16[64,64,128]{2,1,0:T(8,128)(2,1)S(1)} %bitcast.44), channel_id=1, source_target_pairs={{0,2},{1,18},{2,4},{3,20},{4,6},{5,22},{6,8},{7,24},{8,10},{9,26},... | collective-permute-start | bytes 3145736 | tf_op jit(solution)/shard_map/ppermute | solution.py:266
  41.7 70.5 %collective-permute-start.12 = (bf16[64,64,128]{2,1,0:T(8,128)(2,1)S(1)}, bf16[64,64,128]{2,1,0:T(8,128)(2,1)}, u32[]{:S(2)}, u32[]{:S(2)}) collective-permute-start(bf16[64,64,128]{2,1,0:T(8,128)(2,1)S(1)} %bitcast.43), channel_id=1, source_target_pairs={{0,1},{1,0},{2,3},{3,2},{4,5},{5,4},{6,7},{7,6},{8,9},{9,8},{10,11... | collective-permute-start | bytes 3145736 | tf_op jit(solution)/shard_map/ppermute | solution.py:266
  42.3 115.5 %collective-permute-start.11 = (bf16[64,64,128]{2,1,0:T(8,128)(2,1)}, bf16[64,64,128]{2,1,0:T(8,128)(2,1)}, u32[]{:S(2)}, u32[]{:S(2)}) collective-permute-start(bf16[64,64,128]{2,1,0:T(8,128)(2,1)} %bitcast.21), channel_id=1, source_target_pairs={{0,6},{1,22},{2,8},{3,24},{4,10},{5,26},{6,12},{7,28},{8,14},{9,30... | collective-permute-start | bytes 3145736 | tf_op jit(solution)/shard_map/ppermute | solution.py:266
  45.1 112.7 %collective-permute-start.9 = (bf16[64,64,128]{2,1,0:T(8,128)(2,1)}, bf16[64,64,128]{2,1,0:T(8,128)(2,1)}, u32[]{:S(2)}, u32[]{:S(2)}) collective-permute-start(bf16[64,64,128]{2,1,0:T(8,128)(2,1)} %bitcast.19), channel_id=1, source_target_pairs={{0,1},{1,0},{2,3},{3,2},{4,5},{5,4},{6,7},{7,6},{8,9},{9,8},{10,11... | collective-permute-start | bytes 3145736 | tf_op jit(solution)/shard_map/ppermute | solution.py:266
  45.1 112.7 %collective-permute-start.6 = (bf16[64,64,128]{2,1,0:T(8,128)(2,1)}, bf16[64,64,128]{2,1,0:T(8,128)(2,1)}, u32[]{:S(2)}, u32[]{:S(2)}) collective-permute-start(bf16[64,64,128]{2,1,0:T(8,128)(2,1)} %bitcast.45), channel_id=1, source_target_pairs={{0,1},{1,0},{2,3},{3,2},{4,5},{5,4},{6,7},{7,6},{8,9},{9,8},{10,11... | collective-permute-start | bytes 3145736 | tf_op jit(solution)/shard_map/ppermute | solution.py:266
  111.2 1.0 copy-start.5
  112.2 108.3 %collective-permute-start.3 = (bf16[64,64,128]{2,1,0:T(8,128)(2,1)}, bf16[64,64,128]{2,1,0:T(8,128)(2,1)}, u32[]{:S(2)}, u32[]{:S(2)}) collective-permute-start(bf16[64,64,128]{2,1,0:T(8,128)(2,1)} %bitcast.47), channel_id=1, source_target_pairs={{0,1},{1,0},{2,3},{3,2},{4,5},{5,4},{6,7},{7,6},{8,9},{9,8},{10,11... | collective-permute-start | bytes 3145736 | tf_op jit(solution)/shard_map/ppermute | solution.py:266
  112.2 111.8 %collective-permute-start.13 = (bf16[64,64,128]{2,1,0:T(8,128)(2,1)}, bf16[64,64,128]{2,1,0:T(8,128)(2,1)}, u32[]{:S(2)}, u32[]{:S(2)}) collective-permute-start(bf16[64,64,128]{2,1,0:T(8,128)(2,1)} %collective-permute-done.12), channel_id=1, source_target_pairs={{1,0},{0,16},{3,2},{2,18},{5,4},{4,20},{7,6},{6,22},{9,8},{8,24},{... | collective-permute-start | bytes 3145736 | tf_op jit(solution)/shard_map/ppermute | solution.py:266
  157.8 120.7 %collective-permute-start.8 = (bf16[64,64,128]{2,1,0:T(8,128)(2,1)}, bf16[64,64,128]{2,1,0:T(8,128)(2,1)}, u32[]{:S(2)}, u32[]{:S(2)}) collective-permute-start(bf16[64,64,128]{2,1,0:T(8,128)(2,1)} %bitcast.46), channel_id=1, source_target_pairs={{0,10},{1,26},{2,12},{3,28},{4,14},{5,30},{6,0},{7,16},{8,2},{9,18... | collective-permute-start | bytes 3145736 | tf_op jit(solution)/shard_map/ppermute | solution.py:266
  157.8 141.2 %collective-permute-start.5 = (bf16[64,64,128]{2,1,0:T(8,128)(2,1)}, bf16[64,64,128]{2,1,0:T(8,128)(2,1)}, u32[]{:S(2)}, u32[]{:S(2)}) collective-permute-start(bf16[64,64,128]{2,1,0:T(8,128)(2,1)} %bitcast.42), channel_id=1, source_target_pairs={{0,14},{1,30},{2,0},{3,16},{4,2},{5,18},{6,4},{7,20},{8,6},{9,22},... | collective-permute-start | bytes 3145736 | tf_op jit(solution)/shard_map/ppermute | solution.py:266
  157.8 117.2 %collective-permute-start.10 = (bf16[64,64,128]{2,1,0:T(8,128)(2,1)}, bf16[64,64,128]{2,1,0:T(8,128)(2,1)}, u32[]{:S(2)}, u32[]{:S(2)}) collective-permute-start(bf16[64,64,128]{2,1,0:T(8,128)(2,1)} %collective-permute-done.9), channel_id=1, source_target_pairs={{1,4},{0,20},{3,6},{2,22},{5,8},{4,24},{7,10},{6,26},{9,12},{8,28}... | collective-permute-start | bytes 3145736 | tf_op jit(solution)/shard_map/ppermute | solution.py:266
  220.5 75.0 %collective-permute-start.7 = (bf16[64,64,128]{2,1,0:T(8,128)(2,1)}, bf16[64,64,128]{2,1,0:T(8,128)(2,1)}, u32[]{:S(2)}, u32[]{:S(2)}) collective-permute-start(bf16[64,64,128]{2,1,0:T(8,128)(2,1)} %collective-permute-done.6), channel_id=1, source_target_pairs={{1,8},{0,24},{3,10},{2,26},{5,12},{4,28},{7,14},{6,30},{9,0},{8,16... | collective-permute-start | bytes 3145736 | tf_op jit(solution)/shard_map/ppermute | solution.py:266
  224.0 89.0 %collective-permute-start.4 = (bf16[64,64,128]{2,1,0:T(8,128)(2,1)}, bf16[64,64,128]{2,1,0:T(8,128)(2,1)}, u32[]{:S(2)}, u32[]{:S(2)}) collective-permute-start(bf16[64,64,128]{2,1,0:T(8,128)(2,1)} %collective-permute-done.3), channel_id=1, source_target_pairs={{1,12},{0,28},{3,14},{2,30},{5,0},{4,16},{7,2},{6,18},{9,4},{8,20}... | collective-permute-start | bytes 3145736 | tf_op jit(solution)/shard_map/ppermute | solution.py:266
  225.7 1.2 copy-start.6
  229.2 3.6 copy-start.3
  232.7 42.3 %copy-start.4 = (bf16[1,64,64,128]{3,2,1,0:T(8,128)(2,1)S(1)}, bf16[1,64,64,128]{3,2,1,0:T(8,128)(2,1)}, u32[]{:S(2)}) copy-start(bf16[1,64,64,128]{3,2,1,0:T(8,128)(2,1)} %get-tuple-element.30.own) | copy-start | bytes 3145732
  278.5 17.0 %copy-start.2 = (bf16[1,64,64,128]{3,2,1,0:T(8,128)(2,1)S(1)}, bf16[1,64,64,128]{3,2,1,0:T(8,128)(2,1)}, u32[]{:S(2)}) copy-start(bf16[1,64,64,128]{3,2,1,0:T(8,128)(2,1)} %get-tuple-element.33.own) | copy-start | bytes 3145732
  317.9 7.1 %collective-permute-start.15 = (bf16[64,4,128]{2,1,0:T(4,128)(2,1)S(1)}, bf16[64,4,128]{2,1,0:T(4,128)(2,1)S(1)}, u32[]{:S(2)}, u32[]{:S(2)}) collective-permute-start(bf16[64,4,128]{2,1,0:T(4,128)(2,1)S(1)} %slice_select_fusion), channel_id=1, source_target_pairs={{0,1},{1,0},{2,3},{3,2},{4,5},{5,4},{6,7},{7,6},{8,9},{9,8},{10,11... | collective-permute-start | bytes 196616 | tf_op jit(solution)/shard_map/ppermute | solution.py:184
  324.1 7.9 %copy-start.7 = (f32[128]{0:T(128)S(1)}, f32[128]{0:T(128)}, u32[]{:S(2)}) copy-start(f32[128]{0:T(128)} %param.9) | copy-start | bytes 1540
  325.2 24.8 %collective-permute-start.16 = (bf16[4,520,128]{2,1,0:T(8,128)(2,1)S(1)}, bf16[4,520,128]{2,1,0:T(8,128)(2,1)S(1)}, u32[]{:S(2)}, u32[]{:S(2)}) collective-permute-start(bf16[4,520,128]{2,1,0:T(8,128)(2,1)S(1)} %pad_maximum_fusion.4), channel_id=1, source_target_pairs={{0,2},{2,4},{4,6},{6,8},{8,10},{10,12},{12,14},{14,16},{16,18},{18... | collective-permute-start | bytes 1597448 | tf_op jit(solution)/shard_map/ppermute | solution.py:176
  327.2 22.9 %collective-permute-start.17 = (bf16[4,520,128]{2,1,0:T(8,128)(2,1)S(1)}, bf16[4,520,128]{2,1,0:T(8,128)(2,1)S(1)}, u32[]{:S(2)}, u32[]{:S(2)}) collective-permute-start(bf16[4,520,128]{2,1,0:T(8,128)(2,1)S(1)} %pad_maximum_fusion.5), channel_id=1, source_target_pairs={{2,0},{4,2},{6,4},{8,6},{10,8},{12,10},{14,12},{16,14},{18,16},{20... | collective-permute-start | bytes 1597448 | tf_op jit(solution)/shard_map/ppermute | solution.py:176

commit v4 on v2

--- a/solution.py
+++ b/solution.py
@@ -277,14 +277,14 @@
         for s in range(count):
             landed[s] = [(direct(piece(s), s),)]
     else:
-        across = [(device(*p), device(p[0], p[1], 1 - p[2])) for p in places]
         for s in range(count):
             if s % 2:
                 landed[s] = [(direct(piece(s), s),)]
             else:
-                hop = send(piece(s), across)
-                pairs = [(device(a, m, 1 - j), device(j, m + s, a)) for a, m, j in places]
-                landed[s] = [(send(hop, pairs),)]
+                away = [p for p in places if s or p[0] != p[2]]
+                hop = send(piece(s), [(device(*p), device(p[0], p[1], 1 - p[2])) for p in away])
+                pairs = [(device(a, m, 1 - j), device(j, m + s, a)) for a, m, j in away]
+                landed[s] = [(send(hop, pairs),) if s else (send(hop, pairs), piece(0))]
     result = None
     for s in [s for s in range(count) if s in landed] + [s for s in landed if s > 7]:
         i, n = where[-s % count]

time: 340 us -> 322 us (0.947)
  waiting for transfers between devices: 197 us -> 173 us
  starting transfers between devices: 48.2 us -> 53.6 us
    ppermute x12, waiting for transfers between devices: 194 us -> 170 us  [send(): return lax.ppermute(block, ('row', 'col'), pairs)]
    ppermute x12, starting transfers between devices: 35.4 us -> 40.7 us  [send(): return lax.ppermute(block, ('row', 'col'), pairs)]
  transfers between devices with their start and end apart: 18 -> 18, of which waited for: 7 -> 8; matrix products, arithmetic and copies ran while one was open for 2% -> 2% of each run, Pallas kernels for 18% -> 19%
where the time goes in v4:
time: 322 us; the launch traced here: 321 us
  waiting for transfers between devices  173 us (54%)
  Pallas kernels  83.7 us (26%)
  starting transfers between devices  53.6 us (17%)
  local copies, waits for them, and re-layouts  5.61 us (2%)
  other arithmetic  5.27 us (2%)
    ppermute x12, waiting for transfers between devices, send(): return lax.ppermute(block, ('row', 'col'), pairs)  170 us
    ppermute x12, starting transfers between devices, send(): return lax.ppermute(block, ('row', 'col'), pairs)  40.7 us
    pallas_call x2, Pallas kernels, conv(): pl.pallas_call(functools.partial(inner_kernel, finish), grid_spec=pltpu.P...  37.5 us
    pallas_call x8, Pallas kernels, symmetrize(): pl.pallas_call(functools.partial(mirror_kernel, sizes), grid_spec=pltpu.P...  28.5 us
    pallas_call x2, Pallas kernels, conv(): pl.pallas_call(functools.partial(outer_kernel, finish), grid_spec=pltpu.P...  17.7 us
    ppermute x4, starting transfers between devices, move(): lax.ppermute(part, axis, [(i, i + 1) if up else (i + 1, i) for i in range...  11.2 us
  transfers between devices with their start and end apart: 18, of which 8 were waited for; matrix products, arithmetic and copies ran while one was open for 2% of the time, Pallas kernels for 19%

profile of v4, /device:TPU:16, one launch (start us, length us, event | category | flops | bytes accessed | tf_op | source)
XLA Modules:
  0.0 321.4 jit_solution(6656431997477706280)
XLA Ops:
  1.1 1.6 collective-permute-start
  6.0 2.6 collective-permute-start.2
  8.7 1.9 collective-permute-start.1
  10.6 19.5 %shard_map.55 = (bf16[1,64,64,128]{3,2,1,0:T(8,128)(2,1)S(1)}, bf16[1,64,64,128]{3,2,1,0:T(8,128)(2,1)S(1)}, bf16[1,64,64,128]{3,2,1,0:T(8,128)(2,1)S(1)}, bf16[...) custom-call(s32[1]{0:T(128)} %bitcast.me, ...), custom_call_target="tpu_custom_call" | custom-call | flops 9663676416 | bytes 25165824 | tf_op jit(solution)/shard_map/pallas_call | solution.py:109
  31.3 8.7 %shard_map.56 = (bf16[1,64,64,128]{3,2,1,0:T(8,128)(2,1)S(1)}, bf16[1,64,64,128]{3,2,1,0:T(8,128)(2,1)S(1)}, bf16[1,64,64,128]{3,2,1,0:T(8,128)(2,1)S(1)}, bf16[...) custom-call(s32[1]{0:T(128)} %bitcast.me, ...), custom_call_target="tpu_custom_call", output_to_operand_aliasing={{0}: (10, {}), {1}: (11, {}), {2}: (12, {}), {3}: (13, {}),... | custom-call | flops 3221225472 | bytes 8388608 | tf_op jit(solution)/shard_map/pallas_call | solution.py:138
  41.0 3.7 %collective-permute-start.13 = (bf16[64,64,128]{2,1,0:T(8,128)(2,1)S(1)}, bf16[64,64,128]{2,1,0:T(8,128)(2,1)}, u32[]{:S(2)}, u32[]{:S(2)}) collective-permute-start(bf16[64,64,128]{2,1,0:T(8,128)(2,1)S(1)} %bitcast.42), channel_id=1, source_target_pairs={{1,0},{3,2},{5,4},{7,6},{9,8},{11,10},{13,12},{15,14},{16,17},{18,... | collective-permute-start | bytes 3145736 | tf_op jit(solution)/shard_map/ppermute | solution.py:266
  44.7 1.4 collective-permute-start.12
  48.1 18.9 %collective-permute-done.13 = bf16[64,64,128]{2,1,0:T(8,128)(2,1)} collective-permute-done((bf16[64,64,128]{2,1,0:T(8,128)(2,1)S(1)}, bf16[64,64,128]{2,1,0:T(8,128)(2,1)}, u32[]{:S(2)}, u32[]{:S(2)}) %collective-permute-start.13) | collective-permute-done | bytes 1048608 | tf_op jit(solution)/shard_map/ppermute | solution.py:266
  67.1 1.3 collective-permute-start.14
  68.3 25.0 %collective-permute-done.10 = bf16[64,64,128]{2,1,0:T(8,128)(2,1)} collective-permute-done((bf16[64,64,128]{2,1,0:T(8,128)(2,1)S(1)}, bf16[64,64,128]{2,1,0:T(8,128)(2,1)}, u32[]{:S(2)}, u32[]{:S(2)}) %collective-permute-start.10) | collective-permute-done | bytes 1048608 | tf_op jit(solution)/shard_map/ppermute | solution.py:266
  94.2 2.1 collective-permute-start.9
  96.3 36.9 %collective-permute-done.7 = bf16[64,64,128]{2,1,0:T(8,128)(2,1)} collective-permute-done((bf16[64,64,128]{2,1,0:T(8,128)(2,1)}, bf16[64,64,128]{2,1,0:T(8,128)(2,1)}, u32[]{:S(2)}, u32[]{:S(2)}) %collective-permute-start.7) | collective-permute-done | bytes 1048608 | tf_op jit(solution)/shard_map/ppermute | solution.py:266
  133.2 1.3 collective-permute-start.6
  134.5 21.5 %collective-permute-done.4 = bf16[64,64,128]{2,1,0:T(8,128)(2,1)} collective-permute-done((bf16[64,64,128]{2,1,0:T(8,128)(2,1)}, bf16[64,64,128]{2,1,0:T(8,128)(2,1)}, u32[]{:S(2)}, u32[]{:S(2)}) %collective-permute-start.4) | collective-permute-done | bytes 1048608 | tf_op jit(solution)/shard_map/ppermute | solution.py:266
  156.0 24.3 %collective-permute-start.3 = (bf16[64,64,128]{2,1,0:T(8,128)(2,1)}, bf16[64,64,128]{2,1,0:T(8,128)(2,1)}, u32[]{:S(2)}, u32[]{:S(2)}) collective-permute-start(bf16[64,64,128]{2,1,0:T(8,128)(2,1)} %bitcast.50), channel_id=1, source_target_pairs={{0,14},{1,30},{2,0},{3,16},{4,2},{5,18},{6,4},{7,20},{8,6},{9,22},... | collective-permute-start | bytes 3145736 | tf_op jit(solution)/shard_map/ppermute | solution.py:266
  180.3 3.4 %collective-permute-start.8 = (bf16[64,64,128]{2,1,0:T(8,128)(2,1)}, bf16[64,64,128]{2,1,0:T(8,128)(2,1)}, u32[]{:S(2)}, u32[]{:S(2)}) collective-permute-start(bf16[64,64,128]{2,1,0:T(8,128)(2,1)} %collective-permute-done.7), channel_id=1, source_target_pairs={{1,8},{0,24},{3,10},{2,26},{5,12},{4,28},{7,14},{6,30},{9,0},{8,16... | collective-permute-start | bytes 3145736 | tf_op jit(solution)/shard_map/ppermute | solution.py:266
  183.6 1.3 collective-permute-start.5
  186.6 3.8 %shard_map.57.rest_1_ = bf16[64,512,128]{2,1,0:T(8,128)(2,1)} custom-call(s32[2]{0:T(128)S(1)} %pad_add_fusion.7.place, bf16[1,64,64,128]{3,2,1,0:T(8,128)(2,1)S(1)} %get-tuple-element.36.own, bf16[64,64,128]{2,1,0:T(8,128)(2,1)} %collective-permute-done.14.rest_0_, bf16[64,64,128]{2,1,0:T(8,128)(2,1)S(1)} %bitcast.43), custom_call_target="tpu_custom_call" | custom-call | tf_op jit(solution)/shard_map/pallas_call | solution.py:230
  190.4 3.6 %shard_map.58.rest_1_ = bf16[64,512,128]{2,1,0:T(8,128)(2,1)} custom-call(s32[2]{0:T(128)S(1)} %pad_add_fusion.6.place, bf16[1,64,64,128]{3,2,1,0:T(8,128)(2,1)S(1)} %copy-done.6, bf16[64,64,128]{2,1,0:T(8,128)(2,1)} %collective-permute-done.12.rest_0_, bf16[64,512,128]{2,1,0:T(8,128)(2,1)} %shard_map.57.rest_1_), custom_call_target="tpu_custom_call", output_to_operand_aliasing={{}: (3, {})} | custom-call | tf_op jit(solution)/shard_map/pallas_call | solution.py:230
  194.0 3.5 %shard_map.59.rest_1_ = bf16[64,512,128]{2,1,0:T(8,128)(2,1)} custom-call(s32[2]{0:T(128)S(1)} %pad_add_fusion.5.place, bf16[1,64,64,128]{3,2,1,0:T(8,128)(2,1)S(1)} %copy-done.5, bf16[64,64,128]{2,1,0:T(8,128)(2,1)} %collective-permute-done.11.rest_0_, bf16[64,512,128]{2,1,0:T(8,128)(2,1)} %shard_map.58.rest_1_), custom_call_target="tpu_custom_call", output_to_operand_aliasing={{}: (3, {})} | custom-call | tf_op jit(solution)/shard_map/pallas_call | solution.py:230
  197.5 3.5 %shard_map.60.rest_1_ = bf16[64,512,128]{2,1,0:T(8,128)(2,1)} custom-call(s32[2]{0:T(128)S(1)} %pad_add_fusion.4.place, bf16[1,64,64,128]{3,2,1,0:T(8,128)(2,1)S(1)} %copy-done.4, bf16[64,64,128]{2,1,0:T(8,128)(2,1)} %collective-permute-done.9.rest_0_, bf16[64,512,128]{2,1,0:T(8,128)(2,1)} %shard_map.59.rest_1_), custom_call_target="tpu_custom_call", output_to_operand_aliasing={{}: (3, {})} | custom-call | tf_op jit(solution)/shard_map/pallas_call | solution.py:230
  201.1 51.4 %collective-permute-done.8.rest_0_ = bf16[64,64,128]{2,1,0:T(8,128)(2,1)} collective-permute-done((bf16[64,64,128]{2,1,0:T(8,128)(2,1)}, bf16[64,64,128]{2,1,0:T(8,128)(2,1)}, u32[]{:S(2)}, u32[]{:S(2)}) %collective-permute-start.8) | collective-permute-done | bytes 1048608 | tf_op jit(solution)/shard_map/ppermute | solution.py:266
  252.4 3.5 %shard_map.61.rest_1_ = bf16[64,512,128]{2,1,0:T(8,128)(2,1)} custom-call(s32[2]{0:T(128)S(1)} %pad_add_fusion.3.place, bf16[1,64,64,128]{3,2,1,0:T(8,128)(2,1)S(1)} %copy-done.3, bf16[64,64,128]{2,1,0:T(8,128)(2,1)} %collective-permute-done.8.rest_0_, bf16[64,512,128]{2,1,0:T(8,128)(2,1)} %shard_map.60.rest_1_), custom_call_target="tpu_custom_call", output_to_operand_aliasing={{}: (3, {})} | custom-call | tf_op jit(solution)/shard_map/pallas_call | solution.py:230
  256.0 3.5 %shard_map.62.rest_1_ = bf16[64,512,128]{2,1,0:T(8,128)(2,1)} custom-call(s32[2]{0:T(128)S(1)} %pad_add_fusion.2.place, bf16[1,64,64,128]{3,2,1,0:T(8,128)(2,1)S(1)} %copy-done.1, bf16[64,64,128]{2,1,0:T(8,128)(2,1)} %collective-permute-done.6.rest_0_, bf16[64,512,128]{2,1,0:T(8,128)(2,1)} %shard_map.61.rest_1_), custom_call_target="tpu_custom_call", output_to_operand_aliasing={{}: (3, {})} | custom-call | tf_op jit(solution)/shard_map/pallas_call | solution.py:230
  259.5 15.3 %collective-permute-done.5.rest_0_ = bf16[64,64,128]{2,1,0:T(8,128)(2,1)} collective-permute-done((bf16[64,64,128]{2,1,0:T(8,128)(2,1)}, bf16[64,64,128]{2,1,0:T(8,128)(2,1)}, u32[]{:S(2)}, u32[]{:S(2)}) %collective-permute-start.5) | collective-permute-done | bytes 1048608 | tf_op jit(solution)/shard_map/ppermute | solution.py:266
  274.7 3.6 %shard_map.63.rest_1_ = bf16[64,512,128]{2,1,0:T(8,128)(2,1)} custom-call(s32[2]{0:T(128)S(1)} %pad_add_fusion.1.place, bf16[1,64,64,128]{3,2,1,0:T(8,128)(2,1)S(1)} %get-tuple-element.31.own, bf16[64,64,128]{2,1,0:T(8,128)(2,1)} %collective-permute-done.5.rest_0_, bf16[64,512,128]{2,1,0:T(8,128)(2,1)} %shard_map.62.rest_1_), custom_call_target="tpu_custom_call", output_to_operand_aliasing={{}: (3, {})} | custom-call | tf_op jit(solution)/shard_map/pallas_call | solution.py:230
  278.3 3.6 %shard_map.64.one.two.odd.even.rest_0_.three = bf16[64,512,128]{2,1,0:T(8,128)(2,1)} custom-call(s32[2]{0:T(128)S(1)} %pad_add_fusion.place, bf16[1,64,64,128]{3,2,1,0:T(8,128)(2,1)S(1)} %get-tuple-element.29.own, bf16[64,64,128]{2,1,0:T(8,128)(2,1)} %collective-permute-done.3.rest_0_, ...), custom_call_target="tpu_custom_call", output_to_operand_aliasing={{}: (3, {})} | custom-call | tf_op jit(solution)/shard_map/pallas_call | solution.py:230
  284.2 3.0 collective-permute-done.15
  287.3 1.9 collective-permute-start.16
  289.3 4.8 %collective-permute-start.17 = (bf16[4,520,128]{2,1,0:T(8,128)(2,1)S(1)}, bf16[4,520,128]{2,1,0:T(8,128)(2,1)S(1)}, u32[]{:S(2)}, u32[]{:S(2)}) collective-permute-start(bf16[4,520,128]{2,1,0:T(8,128)(2,1)S(1)} %pad_maximum_fusion.5), channel_id=1, source_target_pairs={{2,0},{4,2},{6,4},{8,6},{10,8},{12,10},{14,12},{16,14},{18,16},{20... | collective-permute-start | bytes 1597448 | tf_op jit(solution)/shard_map/ppermute | solution.py:176
  294.1 18.1 %shard_map.65.rest_1_ = bf16[64,512,128]{2,1,0:T(8,128)(2,1)} custom-call(s32[1]{0:T(128)} %bitcast.me, bf16[64,512,128]{2,1,0:T(8,128)(2,1)} %shard_map.64.one.two.odd.even.rest_0_.three, bf16[64,512,128]{2,1,0:T(8,128)(2,1)} %shard_map.64.one.two.odd.even.rest_0_.three, bf16[64,512,128]{2,1,0:T(8,128)(2,1)} %shard_map.64.one.two.odd.even.rest_0_.three, ...), custom_call_target="tpu_custom_call" | custom-call | flops 9663676416 | bytes 25165824 | tf_op jit(solution)/shard_map/pallas_call | solution.py:109
  312.4 9.0 %shard_map.66 = bf16[64,512,128]{2,1,0:T(8,128)(2,1)} custom-call(s32[1]{0:T(128)} %bitcast.me, bf16[4,520,128]{2,1,0:T(8,128)(2,1)S(1)} %collective-permute-done.16.low, bf16[4,520,128]{2,1,0:T(8,128)(2,1)S(1)} %collective-permute-done.17.high, bf16[64,512,128]{2,1,0:T(8,128)(2,1)} %shard_map.64.one.two.odd.even.rest_0_.three, ...), custom_call_target="tpu_custom_call", output_to_operand_aliasing={{}: (11, {})} | custom-call | flops 3221225472 | bytes 8388608 | tf_op jit(solution)/shard_map/pallas_call | solution.py:138
  (83 shorter events, 13.9 us)
Async XLA Ops:
  0.0 3.9 %copy-start.10 = (bf16[3,3,128,128]{3,2,1,0:T(8,128)(2,1)S(1)}, bf16[3,3,128,128]{3,2,1,0:T(8,128)(2,1)}, u32[]{:S(2)}) copy-start(bf16[3,3,128,128]{3,2,1,0:T(8,128)(2,1)} %param.8) | copy-start | bytes 884740
  0.0 3.9 %copy-start.11 = (bf16[3,3,128,128]{3,2,1,0:T(8,128)(2,1)S(1)}, bf16[3,3,128,128]{3,2,1,0:T(8,128)(2,1)}, u32[]{:S(2)}) copy-start(bf16[3,3,128,128]{3,2,1,0:T(8,128)(2,1)} %param.6) | copy-start | bytes 884740
  1.1 4.8 %collective-permute-start = (bf16[64,4,128]{2,1,0:T(4,128)(2,1)S(1)}, bf16[64,4,128]{2,1,0:T(4,128)(2,1)S(1)}, u32[]{:S(2)}, u32[]{:S(2)}) collective-permute-start(bf16[64,4,128]{2,1,0:T(4,128)(2,1)S(1)} %slice_select_fusion.1), channel_id=1, source_target_pairs={{0,1},{1,0},{2,3},{3,2},{4,5},{5,4},{6,7},{7,6},{8,9},{9,8},{10,11... | collective-permute-start | bytes 196616 | tf_op jit(solution)/shard_map/ppermute | solution.py:184
  5.9 4.7 %copy-start.9 = (f32[128]{0:T(128)S(1)}, f32[128]{0:T(128)}, u32[]{:S(2)}) copy-start(f32[128]{0:T(128)} %param.7) | copy-start | bytes 1540
  5.9 4.7 %copy-start.7 = (bf16[1536,256]{1,0:T(8,128)(2,1)S(1)}, bf16[1536,256]{1,0:T(8,128)(2,1)}, u32[]{:S(2)}) copy-start(bf16[1536,256]{1,0:T(8,128)(2,1)} %pad_maximum_fusion.weights) | copy-start | bytes 2359300
  6.0 25.1 %collective-permute-start.2 = (bf16[4,520,128]{2,1,0:T(8,128)(2,1)S(1)}, bf16[4,520,128]{2,1,0:T(8,128)(2,1)S(1)}, u32[]{:S(2)}, u32[]{:S(2)}) collective-permute-start(bf16[4,520,128]{2,1,0:T(8,128)(2,1)S(1)} %pad_maximum_fusion.3), channel_id=1, source_target_pairs={{2,0},{4,2},{6,4},{8,6},{10,8},{12,10},{14,12},{16,14},{18,16},{20... | collective-permute-start | bytes 1597448 | tf_op jit(solution)/shard_map/ppermute | solution.py:176
  8.7 22.5 %collective-permute-start.1 = (bf16[4,520,128]{2,1,0:T(8,128)(2,1)S(1)}, bf16[4,520,128]{2,1,0:T(8,128)(2,1)S(1)}, u32[]{:S(2)}, u32[]{:S(2)}) collective-permute-start(bf16[4,520,128]{2,1,0:T(8,128)(2,1)S(1)} %pad_maximum_fusion.2), channel_id=1, source_target_pairs={{0,2},{2,4},{4,6},{6,8},{8,10},{10,12},{12,14},{14,16},{16,18},{18... | collective-permute-start | bytes 1597448 | tf_op jit(solution)/shard_map/ppermute | solution.py:176
  30.1 1.0 copy-start.2
  40.0 1.0 copy-start
  41.0 26.1 %collective-permute-start.13 = (bf16[64,64,128]{2,1,0:T(8,128)(2,1)S(1)}, bf16[64,64,128]{2,1,0:T(8,128)(2,1)}, u32[]{:S(2)}, u32[]{:S(2)}) collective-permute-start(bf16[64,64,128]{2,1,0:T(8,128)(2,1)S(1)} %bitcast.42), channel_id=1, source_target_pairs={{1,0},{3,2},{5,4},{7,6},{9,8},{11,10},{13,12},{15,14},{16,17},{18,... | collective-permute-start | bytes 3145736 | tf_op jit(solution)/shard_map/ppermute | solution.py:266
  44.7 48.6 %collective-permute-start.10 = (bf16[64,64,128]{2,1,0:T(8,128)(2,1)S(1)}, bf16[64,64,128]{2,1,0:T(8,128)(2,1)}, u32[]{:S(2)}, u32[]{:S(2)}) collective-permute-start(bf16[64,64,128]{2,1,0:T(8,128)(2,1)S(1)} %bitcast.45), channel_id=1, source_target_pairs={{0,1},{1,0},{2,3},{3,2},{4,5},{5,4},{6,7},{7,6},{8,9},{9,8},{10,11... | collective-permute-start | bytes 3145736 | tf_op jit(solution)/shard_map/ppermute | solution.py:266
  44.7 49.5 %collective-permute-start.12 = (bf16[64,64,128]{2,1,0:T(8,128)(2,1)S(1)}, bf16[64,64,128]{2,1,0:T(8,128)(2,1)}, u32[]{:S(2)}, u32[]{:S(2)}) collective-permute-start(bf16[64,64,128]{2,1,0:T(8,128)(2,1)S(1)} %bitcast.44), channel_id=1, source_target_pairs={{0,2},{1,18},{2,4},{3,20},{4,6},{5,22},{6,8},{7,24},{8,10},{9,26},... | collective-permute-start | bytes 3145736 | tf_op jit(solution)/shard_map/ppermute | solution.py:266
  46.1 87.1 %collective-permute-start.7 = (bf16[64,64,128]{2,1,0:T(8,128)(2,1)}, bf16[64,64,128]{2,1,0:T(8,128)(2,1)}, u32[]{:S(2)}, u32[]{:S(2)}) collective-permute-start(bf16[64,64,128]{2,1,0:T(8,128)(2,1)} %bitcast.47), channel_id=1, source_target_pairs={{0,1},{1,0},{2,3},{3,2},{4,5},{5,4},{6,7},{7,6},{8,9},{9,8},{10,11... | collective-permute-start | bytes 3145736 | tf_op jit(solution)/shard_map/ppermute | solution.py:266
  47.3 108.7 %collective-permute-start.4 = (bf16[64,64,128]{2,1,0:T(8,128)(2,1)}, bf16[64,64,128]{2,1,0:T(8,128)(2,1)}, u32[]{:S(2)}, u32[]{:S(2)}) collective-permute-start(bf16[64,64,128]{2,1,0:T(8,128)(2,1)} %bitcast.49), channel_id=1, source_target_pairs={{0,1},{1,0},{2,3},{3,2},{4,5},{5,4},{6,7},{7,6},{8,9},{9,8},{10,11... | collective-permute-start | bytes 3145736 | tf_op jit(solution)/shard_map/ppermute | solution.py:266
  67.1 113.2 %collective-permute-start.14 = (bf16[64,64,128]{2,1,0:T(8,128)(2,1)}, bf16[64,64,128]{2,1,0:T(8,128)(2,1)}, u32[]{:S(2)}, u32[]{:S(2)}) collective-permute-start(bf16[64,64,128]{2,1,0:T(8,128)(2,1)} %collective-permute-done.13), channel_id=1, source_target_pairs={{0,16},{2,18},{4,20},{6,22},{8,24},{10,26},{12,28},{14,30},{17,1},... | collective-permute-start | bytes 3145736 | tf_op jit(solution)/shard_map/ppermute | solution.py:266
  93.3 90.3 %collective-permute-start.11 = (bf16[64,64,128]{2,1,0:T(8,128)(2,1)}, bf16[64,64,128]{2,1,0:T(8,128)(2,1)}, u32[]{:S(2)}, u32[]{:S(2)}) collective-permute-start(bf16[64,64,128]{2,1,0:T(8,128)(2,1)} %collective-permute-done.10), channel_id=1, source_target_pairs={{1,4},{0,20},{3,6},{2,22},{5,8},{4,24},{7,10},{6,26},{9,12},{8,28}... | collective-permute-start | bytes 3145736 | tf_op jit(solution)/shard_map/ppermute | solution.py:266
  94.2 103.3 %collective-permute-start.9 = (bf16[64,64,128]{2,1,0:T(8,128)(2,1)}, bf16[64,64,128]{2,1,0:T(8,128)(2,1)}, u32[]{:S(2)}, u32[]{:S(2)}) collective-permute-start(bf16[64,64,128]{2,1,0:T(8,128)(2,1)} %bitcast.46), channel_id=1, source_target_pairs={{0,6},{1,22},{2,8},{3,24},{4,10},{5,26},{6,12},{7,28},{8,14},{9,30... | collective-permute-start | bytes 3145736 | tf_op jit(solution)/shard_map/ppermute | solution.py:266
  133.2 122.8 %collective-permute-start.6 = (bf16[64,64,128]{2,1,0:T(8,128)(2,1)}, bf16[64,64,128]{2,1,0:T(8,128)(2,1)}, u32[]{:S(2)}, u32[]{:S(2)}) collective-permute-start(bf16[64,64,128]{2,1,0:T(8,128)(2,1)} %bitcast.48), channel_id=1, source_target_pairs={{0,10},{1,26},{2,12},{3,28},{4,14},{5,30},{6,0},{7,16},{8,2},{9,18... | collective-permute-start | bytes 3145736 | tf_op jit(solution)/shard_map/ppermute | solution.py:266
  156.0 122.3 %collective-permute-start.3 = (bf16[64,64,128]{2,1,0:T(8,128)(2,1)}, bf16[64,64,128]{2,1,0:T(8,128)(2,1)}, u32[]{:S(2)}, u32[]{:S(2)}) collective-permute-start(bf16[64,64,128]{2,1,0:T(8,128)(2,1)} %bitcast.50), channel_id=1, source_target_pairs={{0,14},{1,30},{2,0},{3,16},{4,2},{5,18},{6,4},{7,20},{8,6},{9,22},... | collective-permute-start | bytes 3145736 | tf_op jit(solution)/shard_map/ppermute | solution.py:266
  180.3 72.2 %collective-permute-start.8 = (bf16[64,64,128]{2,1,0:T(8,128)(2,1)}, bf16[64,64,128]{2,1,0:T(8,128)(2,1)}, u32[]{:S(2)}, u32[]{:S(2)}) collective-permute-start(bf16[64,64,128]{2,1,0:T(8,128)(2,1)} %collective-permute-done.7), channel_id=1, source_target_pairs={{1,8},{0,24},{3,10},{2,26},{5,12},{4,28},{7,14},{6,30},{9,0},{8,16... | collective-permute-start | bytes 3145736 | tf_op jit(solution)/shard_map/ppermute | solution.py:266
  183.6 91.1 %collective-permute-start.5 = (bf16[64,64,128]{2,1,0:T(8,128)(2,1)}, bf16[64,64,128]{2,1,0:T(8,128)(2,1)}, u32[]{:S(2)}, u32[]{:S(2)}) collective-permute-start(bf16[64,64,128]{2,1,0:T(8,128)(2,1)} %collective-permute-done.4), channel_id=1, source_target_pairs={{1,12},{0,28},{3,14},{2,30},{5,0},{4,16},{7,2},{6,18},{9,4},{8,20}... | collective-permute-start | bytes 3145736 | tf_op jit(solution)/shard_map/ppermute | solution.py:266
  186.6 3.8 %copy-start.6 = (bf16[1,64,64,128]{3,2,1,0:T(8,128)(2,1)S(1)}, bf16[1,64,64,128]{3,2,1,0:T(8,128)(2,1)}, u32[]{:S(2)}) copy-start(bf16[1,64,64,128]{3,2,1,0:T(8,128)(2,1)} %get-tuple-element.30.own) | copy-start | bytes 3145732
  190.4 3.6 %copy-start.5 = (bf16[1,64,64,128]{3,2,1,0:T(8,128)(2,1)S(1)}, bf16[1,64,64,128]{3,2,1,0:T(8,128)(2,1)}, u32[]{:S(2)}) copy-start(bf16[1,64,64,128]{3,2,1,0:T(8,128)(2,1)} %get-tuple-element.32.own) | copy-start | bytes 3145732
  194.0 3.5 %copy-start.4 = (bf16[1,64,64,128]{3,2,1,0:T(8,128)(2,1)S(1)}, bf16[1,64,64,128]{3,2,1,0:T(8,128)(2,1)}, u32[]{:S(2)}) copy-start(bf16[1,64,64,128]{3,2,1,0:T(8,128)(2,1)} %get-tuple-element.34.own) | copy-start | bytes 3145732
  197.5 54.9 %copy-start.3 = (bf16[1,64,64,128]{3,2,1,0:T(8,128)(2,1)S(1)}, bf16[1,64,64,128]{3,2,1,0:T(8,128)(2,1)}, u32[]{:S(2)}) copy-start(bf16[1,64,64,128]{3,2,1,0:T(8,128)(2,1)} %get-tuple-element.35.own) | copy-start | bytes 3145732
  201.1 54.9 %copy-start.1 = (bf16[1,64,64,128]{3,2,1,0:T(8,128)(2,1)S(1)}, bf16[1,64,64,128]{3,2,1,0:T(8,128)(2,1)}, u32[]{:S(2)}) copy-start(bf16[1,64,64,128]{3,2,1,0:T(8,128)(2,1)} %copy-done) | copy-start | bytes 3145732
  282.9 4.3 %collective-permute-start.15 = (bf16[64,4,128]{2,1,0:T(4,128)(2,1)S(1)}, bf16[64,4,128]{2,1,0:T(4,128)(2,1)S(1)}, u32[]{:S(2)}, u32[]{:S(2)}) collective-permute-start(bf16[64,4,128]{2,1,0:T(4,128)(2,1)S(1)} %slice_select_fusion), channel_id=1, source_target_pairs={{0,1},{1,0},{2,3},{3,2},{4,5},{5,4},{6,7},{7,6},{8,9},{9,8},{10,11... | collective-permute-start | bytes 196616 | tf_op jit(solution)/shard_map/ppermute | solution.py:184
  284.2 9.9 %copy-start.8 = (f32[128]{0:T(128)S(1)}, f32[128]{0:T(128)}, u32[]{:S(2)}) copy-start(f32[128]{0:T(128)} %param.9) | copy-start | bytes 1540
  287.3 24.9 %collective-permute-start.16 = (bf16[4,520,128]{2,1,0:T(8,128)(2,1)S(1)}, bf16[4,520,128]{2,1,0:T(8,128)(2,1)S(1)}, u32[]{:S(2)}, u32[]{:S(2)}) collective-permute-start(bf16[4,520,128]{2,1,0:T(8,128)(2,1)S(1)} %pad_maximum_fusion.4), channel_id=1, source_target_pairs={{0,2},{2,4},{4,6},{6,8},{8,10},{10,12},{12,14},{14,16},{16,18},{18... | collective-permute-start | bytes 1597448 | tf_op jit(solution)/shard_map/ppermute | solution.py:176
  289.3 22.9 %collective-permute-start.17 = (bf16[4,520,128]{2,1,0:T(8,128)(2,1)S(1)}, bf16[4,520,128]{2,1,0:T(8,128)(2,1)S(1)}, u32[]{:S(2)}, u32[]{:S(2)}) collective-permute-start(bf16[4,520,128]{2,1,0:T(8,128)(2,1)S(1)} %pad_maximum_fusion.5), channel_id=1, source_target_pairs={{2,0},{4,2},{6,4},{8,6},{10,8},{12,10},{14,12},{16,14},{18,16},{20... | collective-permute-start | bytes 1597448 | tf_op jit(solution)/shard_map/ppermute | solution.py:176
